TPU v7x, 32 devices: a whole 2x2x4 slice. The times are simulated.
32 devices in a mesh: row: 8 (over z, core), col: 4 (over y, x).
Axes of the slice: x: 2, y: 2, z: 4, core: 2. Of those that a mesh axis runs over, the one named last changes fastest.
Arguments:
- pressure_in: float32 [256, 64, 128], P('row', 'col'), may hold values from -6 to 6
- source: float32 [256, 64, 128], P('row', 'col'), may hold values from -18 to 18
- permeability: float32 [256, 64, 128], P('row', 'col'), may hold values from 0.2 to 5
Outputs:
- pressure_out: float32 [256, 64, 128], P('row', 'col')
All inputs are finite; a program needn't handle non-finite values.
Results may differ from a plain program's by a relative error of at most 0.0001.
Values sent between devices are 32-bit elements; how exact they have to be, the bound alone decides.
A program may use at most 128 MiB of HBM per device.

v0:
```python
import jax
import jax.numpy as jnp
from jax import lax
from jax.sharding import PartitionSpec as P

LEVELS = 3
NU1 = 2
NU2 = 2
CSWEEPS = 16


OMEGA = 0.8


def padded_2(array, sides, width):
    for axis, dim in sides:
        size, length = (lax.axis_size(axis), array.shape[dim])
        up = [(i, (i + 1) % size) for i in range(size)]
        down = [(j, i) for i, j in up]
        last = lax.slice_in_dim(array, length - width, length, axis=dim)
        first = lax.slice_in_dim(array, 0, width, axis=dim)
        before = lax.ppermute(last, axis, up)
        after = lax.ppermute(first, axis, down)
        array = jnp.concatenate([before, array, after], axis=dim)
    return array


def harmonic(left, right, scale):
    return 2.0 * left * right / (left + right) * scale


def coefficients(padded, center, scale):
    west_x = harmonic(padded[:-2, 1:-1], center, scale)
    east_x = harmonic(center, padded[2:, 1:-1], scale)
    west_y = harmonic(padded[1:-1, :-2], center, scale)
    east_y = harmonic(center, padded[1:-1, 2:], scale)
    inner = harmonic(center[:, :, :-1], center[:, :, 1:], scale)
    below = jnp.concatenate([2.0 * center[:, :, :1] * scale, inner], axis=2)
    above = jnp.concatenate([inner, 2.0 * center[:, :, -1:] * scale], axis=2)
    diagonal = west_x + east_x + west_y + east_y + below + above
    return (west_x, east_x, west_y, east_y, below, above, diagonal)


def apply_operator(padded, center, faces):
    west_x, east_x, west_y, east_y, below, above, diagonal = faces
    zero_plane = jnp.zeros_like(center[:, :, :1])
    under = jnp.concatenate([zero_plane, center[:, :, :-1]], axis=2)
    over = jnp.concatenate([center[:, :, 1:], zero_plane], axis=2)
    beside_all = west_x * padded[:-2, 1:-1] + east_x * padded[2:, 1:-1]
    beside_all = beside_all + west_y * padded[1:-1, :-2] + east_y * padded[1:-1, 2:]
    beside_all = beside_all + below * under + above * over
    return diagonal * center - beside_all


def jacobi_sweep(pressure, right_side, faces, padder):
    return (
        pressure
        + OMEGA * (right_side - apply_operator(padder(pressure), pressure, faces)) / faces[6]
    )


def first_sweep(right_side, faces):
    return OMEGA * right_side / faces[6]


def coarsen(field):
    size_x, size_y, size_z = field.shape
    return field.reshape(size_x // 2, 2, size_y // 2, 2, size_z // 2, 2).mean(axis=(1, 3, 5))


def prolong(field):
    return jnp.repeat(jnp.repeat(jnp.repeat(field, 2, axis=0), 2, axis=1), 2, axis=2)


def mesh_pad(field):
    return padded_2(field, (("row", 0), ("col", 1)), 1)


def perm_pad(field):
    return padded_2(field, (("row", 0), ("col", 1)), 1)


def band_pad(field):
    extended = padded_2(field, (("row", 0),), 1)
    return jnp.pad(extended, ((0, 0), (1, 1), (0, 0)), mode="wrap")


def band_perm_pad(field):
    extended = padded_2(field, (("row", 0),), 1)
    return jnp.pad(extended, ((0, 0), (1, 1), (0, 0)), mode="wrap")


def coarse_solve(right_side, faces, padder):
    start = first_sweep(right_side, faces)

    def one_sweep(sweep_index, current):
        return jacobi_sweep(current, right_side, faces, padder)

    return lax.fori_loop(1, CSWEEPS, one_sweep, start)


def on_device(pressure_in, source, permeability):
    perms = [permeability]
    for depth_level in range(LEVELS):
        perms.append(coarsen(perms[depth_level]))
    pressure = pressure_in
    right_side = source
    states = []
    all_faces = [
        coefficients(perm_pad(perms[depth_level]), perms[depth_level], 0.25**depth_level)
        for depth_level in range(LEVELS)
    ]
    for depth_level in range(LEVELS):
        faces = all_faces[depth_level]
        if depth_level == 0:
            for sweep_index in range(NU1):
                pressure = jacobi_sweep(pressure, right_side, faces, mesh_pad)
        else:
            pressure = first_sweep(right_side, faces)
            pressure = jacobi_sweep(pressure, right_side, faces, mesh_pad)
        states.append((pressure, right_side))
        residual = right_side - apply_operator(mesh_pad(pressure), pressure, faces)
        right_side = coarsen(residual)
    coarse_perm = perms[LEVELS]
    size_x, size_y, size_z = right_side.shape
    coarse_scale = 0.25**LEVELS
    band_rhs, band_perm = (
        lax.all_gather(right_side, "col", axis=1, tiled=True),
        lax.all_gather(coarse_perm, "col", axis=1, tiled=True),
    )
    band_faces = coefficients(band_perm_pad(band_perm), band_perm, coarse_scale)
    solved = coarse_solve(band_rhs, band_faces, band_pad)
    correction = lax.dynamic_slice_in_dim(solved, lax.axis_index("col") * size_y, size_y, 1)
    for depth_level in range(LEVELS - 1, -1, -1):
        pressure, right_side = states[depth_level]
        pressure = pressure + prolong(correction)
        for sweep_index in range(NU2):
            pressure = jacobi_sweep(pressure, right_side, all_faces[depth_level], mesh_pad)
        correction = pressure
    return correction


def solution(mesh):
    placed = (P("row", "col", None), P("row", "col", None), P("row", "col", None))
    return jax.shard_map(
        on_device, mesh=mesh, in_specs=placed, out_specs=P("row", "col", None), check_vma=False
    )
```

profile of v0, /device:TPU:0, one launch (start us, length us, event | category | flops | bytes accessed | tf_op | source)
XLA Modules:
  0.0 323.5 jit_solution(6088923386562765389)
XLA Ops:
  1.2 4.0 %collective-permute-start.3 = (f32[1,16,128]{2,1,0:T(8,128)S(1)}, f32[1,16,128]{2,1,0:T(8,128)S(1)}, u32[]{:S(2)}, u32[]{:S(2)}) collective-permute-start(f32[1,16,128]{2,1,0:T(8,128)S(1)} %get-tuple-element.167), channel_id=1, source_target_pairs={{4,0},{8,4},{12,8},{16,12},{20,16},{24,20},{28,24},{0,28},{5,1},{9... | collective-permute-start | bytes 24584 | tf_op jit(solution)/shard_map/ppermute | solution.py:23
  5.9 3.5 %collective-permute-start.7 = (f32[1,16,128]{2,1,0:T(8,128)S(1)}, f32[1,16,128]{2,1,0:T(8,128)S(1)}, u32[]{:S(2)}, u32[]{:S(2)}) collective-permute-start(f32[1,16,128]{2,1,0:T(8,128)S(1)} %get-tuple-element.171), channel_id=1, source_target_pairs={{4,0},{8,4},{12,8},{16,12},{20,16},{24,20},{28,24},{0,28},{5,1},{9... | collective-permute-start | bytes 24584 | tf_op jit(solution)/shard_map/ppermute | solution.py:23
  13.6 18.9 %reshape.48 = f32[16,2,8,2,64,2]{5,4,3,2,1,0:T(8,128)} reshape(f32[32,16,128]{2,1,0:T(8,128)} %param.7) | data formatting | bytes 524288 | tf_op jit(solution)/shard_map/reshape | solution.py:68
  32.5 7.0 %reduce_sum.55 = f32[16,8,64]{2,1,0:T(8,128)S(1)} reduce(f32[16,2,8,2,64,2]{5,4,3,2,1,0:T(8,128)} %reshape.48, f32[]{:T(128)} %constant.23.clone.1), dimensions={1,3,5}, to_apply=%region_1.0 | reduce | flops 57344 | bytes 294916 | tf_op jit(solution)/shard_map/reduce_sum | solution.py:68
  44.4 8.7 %all_gather.7 = f32[4,8,16]{2,0,1:T(4,128)S(1)} all-gather(f32[4,2,16]{2,0,1:T(4,128)S(1)} %broadcast_multiply_fusion.2), channel_id=1, replica_groups=mesh['row'=8,'col'=4] {'col'}, dimensions={1}, use_global_device_ids=true | all-gather | bytes 2560 | tf_op jit(solution)/shard_map/all_gather | solution.py:129
  91.5 18.1 %reshape.47 = f32[16,2,8,2,64,2]{5,4,3,2,1,0:T(8,128)} reshape(f32[32,16,128]{2,1,0:T(8,128)S(1)} %fusion.47) | data formatting | bytes 524288 | tf_op jit(solution)/shard_map/reshape | solution.py:68
  109.7 7.0 %reduce_sum.54 = f32[16,8,64]{2,1,0:T(8,128)S(1)} reduce(f32[16,2,8,2,64,2]{5,4,3,2,1,0:T(8,128)} %reshape.47, f32[]{:T(128)} %constant.23.clone.1), dimensions={1,3,5}, to_apply=%region_0.0 | reduce | flops 57344 | bytes 294916 | tf_op jit(solution)/shard_map/reduce_sum | solution.py:68
  168.5 7.6 %all_gather.6 = f32[4,8,16]{2,0,1:T(4,128)S(1)} all-gather(f32[4,2,16]{2,0,1:T(4,128)S(1)} %broadcast_multiply_fusion.3), channel_id=1, replica_groups=mesh['row'=8,'col'=4] {'col'}, dimensions={1}, use_global_device_ids=true | all-gather | bytes 2560 | tf_op jit(solution)/shard_map/all_gather | solution.py:128
  177.3 75.8 %while.10 = (s32[]{:T(128)}, f32[4,8,16]{2,1,0:T(8,128)S(1)}, f32[4,8,16]{2,1,0:T(8,128)S(1)}, f32[4,8,16]{2,1,0:T(8,128)S(1)}, f32[4,8,16]{2,1,0:T(8,128)S(1)},...) while((s32[]{:T(128)}, f32[4,8,16]{2,1,0:T(8,128)S(1)}, ...), condition=%wide.region_7.8_spmd, body=%wide.region_6.7_spmd.sunk | while | flops 10754 | bytes 94397 | solution.py:99
  182.4 3.6 %collective-permute-start.1 = (f32[1,8,16]{2,1,0:T(8,128)S(1)}, f32[1,8,16]{2,1,0:T(8,128)S(1)}, u32[]{:S(2)}, u32[]{:S(2)}) collective-permute-start(f32[1,8,16]{2,1,0:T(8,128)S(1)} %get-tuple-element.306), channel_id=1, source_target_pairs={{4,0},{8,4},{12,8},{16,12},{20,16},{24,20},{28,24},{0,28},{5,1},{9... | collective-permute-start | bytes 1544 | tf_op jit(solution)/shard_map/while/body/eval_jaxpr/ppermute | solution.py:23
  187.5 3.6 %collective-permute-start.1 = (f32[1,8,16]{2,1,0:T(8,128)S(1)}, f32[1,8,16]{2,1,0:T(8,128)S(1)}, u32[]{:S(2)}, u32[]{:S(2)}) collective-permute-start(f32[1,8,16]{2,1,0:T(8,128)S(1)} %get-tuple-element.306), channel_id=1, source_target_pairs={{4,0},{8,4},{12,8},{16,12},{20,16},{24,20},{28,24},{0,28},{5,1},{9... | collective-permute-start | bytes 1544 | tf_op jit(solution)/shard_map/while/body/eval_jaxpr/ppermute | solution.py:23
  192.5 3.6 %collective-permute-start.1 = (f32[1,8,16]{2,1,0:T(8,128)S(1)}, f32[1,8,16]{2,1,0:T(8,128)S(1)}, u32[]{:S(2)}, u32[]{:S(2)}) collective-permute-start(f32[1,8,16]{2,1,0:T(8,128)S(1)} %get-tuple-element.306), channel_id=1, source_target_pairs={{4,0},{8,4},{12,8},{16,12},{20,16},{24,20},{28,24},{0,28},{5,1},{9... | collective-permute-start | bytes 1544 | tf_op jit(solution)/shard_map/while/body/eval_jaxpr/ppermute | solution.py:23
  197.6 3.6 %collective-permute-start.1 = (f32[1,8,16]{2,1,0:T(8,128)S(1)}, f32[1,8,16]{2,1,0:T(8,128)S(1)}, u32[]{:S(2)}, u32[]{:S(2)}) collective-permute-start(f32[1,8,16]{2,1,0:T(8,128)S(1)} %get-tuple-element.306), channel_id=1, source_target_pairs={{4,0},{8,4},{12,8},{16,12},{20,16},{24,20},{28,24},{0,28},{5,1},{9... | collective-permute-start | bytes 1544 | tf_op jit(solution)/shard_map/while/body/eval_jaxpr/ppermute | solution.py:23
  202.6 3.6 %collective-permute-start.1 = (f32[1,8,16]{2,1,0:T(8,128)S(1)}, f32[1,8,16]{2,1,0:T(8,128)S(1)}, u32[]{:S(2)}, u32[]{:S(2)}) collective-permute-start(f32[1,8,16]{2,1,0:T(8,128)S(1)} %get-tuple-element.306), channel_id=1, source_target_pairs={{4,0},{8,4},{12,8},{16,12},{20,16},{24,20},{28,24},{0,28},{5,1},{9... | collective-permute-start | bytes 1544 | tf_op jit(solution)/shard_map/while/body/eval_jaxpr/ppermute | solution.py:23
  207.7 3.6 %collective-permute-start.1 = (f32[1,8,16]{2,1,0:T(8,128)S(1)}, f32[1,8,16]{2,1,0:T(8,128)S(1)}, u32[]{:S(2)}, u32[]{:S(2)}) collective-permute-start(f32[1,8,16]{2,1,0:T(8,128)S(1)} %get-tuple-element.306), channel_id=1, source_target_pairs={{4,0},{8,4},{12,8},{16,12},{20,16},{24,20},{28,24},{0,28},{5,1},{9... | collective-permute-start | bytes 1544 | tf_op jit(solution)/shard_map/while/body/eval_jaxpr/ppermute | solution.py:23
  212.8 3.6 %collective-permute-start.1 = (f32[1,8,16]{2,1,0:T(8,128)S(1)}, f32[1,8,16]{2,1,0:T(8,128)S(1)}, u32[]{:S(2)}, u32[]{:S(2)}) collective-permute-start(f32[1,8,16]{2,1,0:T(8,128)S(1)} %get-tuple-element.306), channel_id=1, source_target_pairs={{4,0},{8,4},{12,8},{16,12},{20,16},{24,20},{28,24},{0,28},{5,1},{9... | collective-permute-start | bytes 1544 | tf_op jit(solution)/shard_map/while/body/eval_jaxpr/ppermute | solution.py:23
  217.8 3.6 %collective-permute-start.1 = (f32[1,8,16]{2,1,0:T(8,128)S(1)}, f32[1,8,16]{2,1,0:T(8,128)S(1)}, u32[]{:S(2)}, u32[]{:S(2)}) collective-permute-start(f32[1,8,16]{2,1,0:T(8,128)S(1)} %get-tuple-element.306), channel_id=1, source_target_pairs={{4,0},{8,4},{12,8},{16,12},{20,16},{24,20},{28,24},{0,28},{5,1},{9... | collective-permute-start | bytes 1544 | tf_op jit(solution)/shard_map/while/body/eval_jaxpr/ppermute | solution.py:23
  222.9 3.6 %collective-permute-start.1 = (f32[1,8,16]{2,1,0:T(8,128)S(1)}, f32[1,8,16]{2,1,0:T(8,128)S(1)}, u32[]{:S(2)}, u32[]{:S(2)}) collective-permute-start(f32[1,8,16]{2,1,0:T(8,128)S(1)} %get-tuple-element.306), channel_id=1, source_target_pairs={{4,0},{8,4},{12,8},{16,12},{20,16},{24,20},{28,24},{0,28},{5,1},{9... | collective-permute-start | bytes 1544 | tf_op jit(solution)/shard_map/while/body/eval_jaxpr/ppermute | solution.py:23
  227.9 3.6 %collective-permute-start.1 = (f32[1,8,16]{2,1,0:T(8,128)S(1)}, f32[1,8,16]{2,1,0:T(8,128)S(1)}, u32[]{:S(2)}, u32[]{:S(2)}) collective-permute-start(f32[1,8,16]{2,1,0:T(8,128)S(1)} %get-tuple-element.306), channel_id=1, source_target_pairs={{4,0},{8,4},{12,8},{16,12},{20,16},{24,20},{28,24},{0,28},{5,1},{9... | collective-permute-start | bytes 1544 | tf_op jit(solution)/shard_map/while/body/eval_jaxpr/ppermute | solution.py:23
  233.0 3.6 %collective-permute-start.1 = (f32[1,8,16]{2,1,0:T(8,128)S(1)}, f32[1,8,16]{2,1,0:T(8,128)S(1)}, u32[]{:S(2)}, u32[]{:S(2)}) collective-permute-start(f32[1,8,16]{2,1,0:T(8,128)S(1)} %get-tuple-element.306), channel_id=1, source_target_pairs={{4,0},{8,4},{12,8},{16,12},{20,16},{24,20},{28,24},{0,28},{5,1},{9... | collective-permute-start | bytes 1544 | tf_op jit(solution)/shard_map/while/body/eval_jaxpr/ppermute | solution.py:23
  238.0 3.6 %collective-permute-start.1 = (f32[1,8,16]{2,1,0:T(8,128)S(1)}, f32[1,8,16]{2,1,0:T(8,128)S(1)}, u32[]{:S(2)}, u32[]{:S(2)}) collective-permute-start(f32[1,8,16]{2,1,0:T(8,128)S(1)} %get-tuple-element.306), channel_id=1, source_target_pairs={{4,0},{8,4},{12,8},{16,12},{20,16},{24,20},{28,24},{0,28},{5,1},{9... | collective-permute-start | bytes 1544 | tf_op jit(solution)/shard_map/while/body/eval_jaxpr/ppermute | solution.py:23
  243.1 3.6 %collective-permute-start.1 = (f32[1,8,16]{2,1,0:T(8,128)S(1)}, f32[1,8,16]{2,1,0:T(8,128)S(1)}, u32[]{:S(2)}, u32[]{:S(2)}) collective-permute-start(f32[1,8,16]{2,1,0:T(8,128)S(1)} %get-tuple-element.306), channel_id=1, source_target_pairs={{4,0},{8,4},{12,8},{16,12},{20,16},{24,20},{28,24},{0,28},{5,1},{9... | collective-permute-start | bytes 1544 | tf_op jit(solution)/shard_map/while/body/eval_jaxpr/ppermute | solution.py:23
  248.1 3.6 %collective-permute-start.1 = (f32[1,8,16]{2,1,0:T(8,128)S(1)}, f32[1,8,16]{2,1,0:T(8,128)S(1)}, u32[]{:S(2)}, u32[]{:S(2)}) collective-permute-start(f32[1,8,16]{2,1,0:T(8,128)S(1)} %get-tuple-element.306), channel_id=1, source_target_pairs={{4,0},{8,4},{12,8},{16,12},{20,16},{24,20},{28,24},{0,28},{5,1},{9... | collective-permute-start | bytes 1544 | tf_op jit(solution)/shard_map/while/body/eval_jaxpr/ppermute | solution.py:23
  253.4 3.6 %collective-permute-start.45 = (f32[1,4,32]{2,1,0:T(4,128)S(1)}, f32[1,4,32]{2,1,0:T(4,128)S(1)}, u32[]{:S(2)}, u32[]{:S(2)}) collective-permute-start(f32[1,4,32]{2,1,0:T(4,128)S(1)} %get-tuple-element.220), channel_id=1, source_target_pairs={{4,0},{8,4},{12,8},{16,12},{20,16},{24,20},{28,24},{0,28},{5,1},{9... | collective-permute-start | bytes 1544 | tf_op jit(solution)/shard_map/ppermute | solution.py:23
  (470 shorter events, 193.9 us)
Async XLA Ops:
  0.7 53.7 %collective-permute-start.2 = (f32[1,16,128]{2,1,0:T(8,128)S(1)}, f32[1,16,128]{2,1,0:T(8,128)S(1)}, u32[]{:S(2)}, u32[]{:S(2)}) collective-permute-start(f32[1,16,128]{2,1,0:T(8,128)S(1)} %get-tuple-element.168), channel_id=1, source_target_pairs={{0,4},{4,8},{8,12},{12,16},{16,20},{20,24},{24,28},{28,0},{1,5},{5... | collective-permute-start | bytes 24584 | tf_op jit(solution)/shard_map/ppermute | solution.py:22
  1.2 53.3 %collective-permute-start.3 = (f32[1,16,128]{2,1,0:T(8,128)S(1)}, f32[1,16,128]{2,1,0:T(8,128)S(1)}, u32[]{:S(2)}, u32[]{:S(2)}) collective-permute-start(f32[1,16,128]{2,1,0:T(8,128)S(1)} %get-tuple-element.167), channel_id=1, source_target_pairs={{4,0},{8,4},{12,8},{16,12},{20,16},{24,20},{28,24},{0,28},{5,1},{9... | collective-permute-start | bytes 24584 | tf_op jit(solution)/shard_map/ppermute | solution.py:23
  5.9 51.5 %collective-permute-start.6 = (f32[1,16,128]{2,1,0:T(8,128)S(1)}, f32[1,16,128]{2,1,0:T(8,128)S(1)}, u32[]{:S(2)}, u32[]{:S(2)}) collective-permute-start(f32[1,16,128]{2,1,0:T(8,128)S(1)} %get-tuple-element.172), channel_id=1, source_target_pairs={{0,4},{4,8},{8,12},{12,16},{16,20},{20,24},{24,28},{28,0},{1,5},{5... | collective-permute-start | bytes 24584 | tf_op jit(solution)/shard_map/ppermute | solution.py:22
  5.9 51.6 %collective-permute-start.7 = (f32[1,16,128]{2,1,0:T(8,128)S(1)}, f32[1,16,128]{2,1,0:T(8,128)S(1)}, u32[]{:S(2)}, u32[]{:S(2)}) collective-permute-start(f32[1,16,128]{2,1,0:T(8,128)S(1)} %get-tuple-element.171), channel_id=1, source_target_pairs={{4,0},{8,4},{12,8},{16,12},{20,16},{24,20},{28,24},{0,28},{5,1},{9... | collective-permute-start | bytes 24584 | tf_op jit(solution)/shard_map/ppermute | solution.py:23
  54.5 6.1 %collective-permute-start.4 = (f32[34,1,128]{2,1,0:T(1,128)S(1)}, f32[34,1,128]{2,1,0:T(1,128)S(1)}, u32[]{:S(2)}, u32[]{:S(2)}) collective-permute-start(f32[34,1,128]{2,1,0:T(1,128)S(1)} %get-tuple-element.146), channel_id=1, source_target_pairs={{0,1},{1,2},{2,3},{3,0},{4,5},{5,6},{6,7},{7,4},{8,9},{9,10},{10,1... | collective-permute-start | bytes 52232 | tf_op jit(solution)/shard_map/ppermute | solution.py:22
  56.0 8.1 %collective-permute-start.5 = (f32[34,1,128]{2,1,0:T(1,128)S(1)}, f32[34,1,128]{2,1,0:T(1,128)S(1)}, u32[]{:S(2)}, u32[]{:S(2)}) collective-permute-start(f32[34,1,128]{2,1,0:T(1,128)S(1)} %get-tuple-element.145), channel_id=1, source_target_pairs={{1,0},{2,1},{3,2},{0,3},{5,4},{6,5},{7,6},{4,7},{9,8},{10,9},{11,1... | collective-permute-start | bytes 52232 | tf_op jit(solution)/shard_map/ppermute | solution.py:23
  57.6 6.5 %collective-permute-start.8 = (f32[34,1,128]{2,1,0:T(1,128)S(1)}, f32[34,1,128]{2,1,0:T(1,128)S(1)}, u32[]{:S(2)}, u32[]{:S(2)}) collective-permute-start(f32[34,1,128]{2,1,0:T(1,128)S(1)} %get-tuple-element.147), channel_id=1, source_target_pairs={{0,1},{1,2},{2,3},{3,0},{4,5},{5,6},{6,7},{7,4},{8,9},{9,10},{10,1... | collective-permute-start | bytes 52232 | tf_op jit(solution)/shard_map/ppermute | solution.py:22
  58.2 5.9 %collective-permute-start.9 = (f32[34,1,128]{2,1,0:T(1,128)S(1)}, f32[34,1,128]{2,1,0:T(1,128)S(1)}, u32[]{:S(2)}, u32[]{:S(2)}) collective-permute-start(f32[34,1,128]{2,1,0:T(1,128)S(1)} %get-tuple-element.148), channel_id=1, source_target_pairs={{1,0},{2,1},{3,2},{0,3},{5,4},{6,5},{7,6},{4,7},{9,8},{10,9},{11,1... | collective-permute-start | bytes 52232 | tf_op jit(solution)/shard_map/ppermute | solution.py:23
  60.6 18.9 %collective-permute-start.18 = (f32[1,8,64]{2,1,0:T(8,128)S(1)}, f32[1,8,64]{2,1,0:T(8,128)S(1)}, u32[]{:S(2)}, u32[]{:S(2)}) collective-permute-start(f32[1,8,64]{2,1,0:T(8,128)S(1)} %get-tuple-element.202), channel_id=1, source_target_pairs={{0,4},{4,8},{8,12},{12,16},{16,20},{20,24},{24,28},{28,0},{1,5},{5... | collective-permute-start | bytes 6152 | tf_op jit(solution)/shard_map/ppermute | solution.py:22
  60.6 22.4 %collective-permute-start.19 = (f32[1,8,64]{2,1,0:T(8,128)S(1)}, f32[1,8,64]{2,1,0:T(8,128)S(1)}, u32[]{:S(2)}, u32[]{:S(2)}) collective-permute-start(f32[1,8,64]{2,1,0:T(8,128)S(1)} %get-tuple-element.201), channel_id=1, source_target_pairs={{4,0},{8,4},{12,8},{16,12},{20,16},{24,20},{28,24},{0,28},{5,1},{9... | collective-permute-start | bytes 6152 | tf_op jit(solution)/shard_map/ppermute | solution.py:23
  66.2 4.9 %collective-permute-start.10 = (f32[1,16,128]{2,1,0:T(8,128)S(1)}, f32[1,16,128]{2,1,0:T(8,128)S(1)}, u32[]{:S(2)}, u32[]{:S(2)}) collective-permute-start(f32[1,16,128]{2,1,0:T(8,128)S(1)} %get-tuple-element.163), channel_id=1, source_target_pairs={{0,4},{4,8},{8,12},{12,16},{16,20},{20,24},{24,28},{28,0},{1,5},{5... | collective-permute-start | bytes 24584 | tf_op jit(solution)/shard_map/ppermute | solution.py:22
  72.3 5.9 %collective-permute-start.13 = (f32[34,1,128]{2,1,0:T(1,128)S(1)}, f32[34,1,128]{2,1,0:T(1,128)S(1)}, u32[]{:S(2)}, u32[]{:S(2)}) collective-permute-start(f32[34,1,128]{2,1,0:T(1,128)S(1)} %get-tuple-element.144), channel_id=1, source_target_pairs={{1,0},{2,1},{3,2},{0,3},{5,4},{6,5},{7,6},{4,7},{9,8},{10,9},{11,1... | collective-permute-start | bytes 52232 | tf_op jit(solution)/shard_map/ppermute | solution.py:23
  74.3 54.8 %collective-permute-start.30 = (f32[1,4,32]{2,1,0:T(4,128)S(1)}, f32[1,4,32]{2,1,0:T(4,128)S(1)}, u32[]{:S(2)}, u32[]{:S(2)}) collective-permute-start(f32[1,4,32]{2,1,0:T(4,128)S(1)} %get-tuple-element.236), channel_id=1, source_target_pairs={{0,4},{4,8},{8,12},{12,16},{16,20},{20,24},{24,28},{28,0},{1,5},{5... | collective-permute-start | bytes 1544 | tf_op jit(solution)/shard_map/ppermute | solution.py:22
  75.9 56.7 %collective-permute-start.31 = (f32[1,4,32]{2,1,0:T(4,128)S(1)}, f32[1,4,32]{2,1,0:T(4,128)S(1)}, u32[]{:S(2)}, u32[]{:S(2)}) collective-permute-start(f32[1,4,32]{2,1,0:T(4,128)S(1)} %get-tuple-element.235), channel_id=1, source_target_pairs={{4,0},{8,4},{12,8},{16,12},{20,16},{24,20},{28,24},{0,28},{5,1},{9... | collective-permute-start | bytes 1544 | tf_op jit(solution)/shard_map/ppermute | solution.py:23
  79.3 4.9 %collective-permute-start.14 = (f32[1,16,128]{2,1,0:T(8,128)S(1)}, f32[1,16,128]{2,1,0:T(8,128)S(1)}, u32[]{:S(2)}, u32[]{:S(2)}) collective-permute-start(f32[1,16,128]{2,1,0:T(8,128)S(1)} %get-tuple-element.159), channel_id=1, source_target_pairs={{0,4},{4,8},{8,12},{12,16},{16,20},{20,24},{24,28},{28,0},{1,5},{5... | collective-permute-start | bytes 24584 | tf_op jit(solution)/shard_map/ppermute | solution.py:22
  85.0 5.5 %collective-permute-start.17 = (f32[34,1,128]{2,1,0:T(1,128)S(1)}, f32[34,1,128]{2,1,0:T(1,128)S(1)}, u32[]{:S(2)}, u32[]{:S(2)}) collective-permute-start(f32[34,1,128]{2,1,0:T(1,128)S(1)} %get-tuple-element.142), channel_id=1, source_target_pairs={{1,0},{2,1},{3,2},{0,3},{5,4},{6,5},{7,6},{4,7},{9,8},{10,9},{11,1... | collective-permute-start | bytes 52232 | tf_op jit(solution)/shard_map/ppermute | solution.py:23
  87.5 29.2 %collective-permute-start.20 = (f32[18,1,64]{2,1,0:T(1,128)S(1)}, f32[18,1,64]{2,1,0:T(1,128)S(1)}, u32[]{:S(2)}, u32[]{:S(2)}) collective-permute-start(f32[18,1,64]{2,1,0:T(1,128)S(1)} %get-tuple-element.182), channel_id=1, source_target_pairs={{0,1},{1,2},{2,3},{3,0},{4,5},{5,6},{6,7},{7,4},{8,9},{9,10},{10,1... | collective-permute-start | bytes 13832 | tf_op jit(solution)/shard_map/ppermute | solution.py:22
  89.0 27.6 %collective-permute-start.21 = (f32[18,1,64]{2,1,0:T(1,128)S(1)}, f32[18,1,64]{2,1,0:T(1,128)S(1)}, u32[]{:S(2)}, u32[]{:S(2)}) collective-permute-start(f32[18,1,64]{2,1,0:T(1,128)S(1)} %get-tuple-element.181), channel_id=1, source_target_pairs={{1,0},{2,1},{3,2},{0,3},{5,4},{6,5},{7,6},{4,7},{9,8},{10,9},{11,1... | collective-permute-start | bytes 13832 | tf_op jit(solution)/shard_map/ppermute | solution.py:23
  123.5 5.4 %collective-permute-start.25 = (f32[18,1,64]{2,1,0:T(1,128)S(1)}, f32[18,1,64]{2,1,0:T(1,128)S(1)}, u32[]{:S(2)}, u32[]{:S(2)}) collective-permute-start(f32[18,1,64]{2,1,0:T(1,128)S(1)} %get-tuple-element.180), channel_id=1, source_target_pairs={{1,0},{2,1},{3,2},{0,3},{5,4},{6,5},{7,6},{4,7},{9,8},{10,9},{11,1... | collective-permute-start | bytes 13832 | tf_op jit(solution)/shard_map/ppermute | solution.py:23
  124.9 51.2 %collective-permute-start.42 = (f32[1,8,16]{2,0,1:T(1,128)}, f32[1,8,16]{2,0,1:T(1,128)}, u32[]{:S(2)}, u32[]{:S(2)}) collective-permute-start(f32[1,8,16]{2,0,1:T(1,128)} %get-tuple-element.223), channel_id=1, source_target_pairs={{0,4},{4,8},{8,12},{12,16},{16,20},{20,24},{24,28},{28,0},{1,5},{5... | collective-permute-start | bytes 1544 | tf_op jit(solution)/shard_map/ppermute | solution.py:22
  126.5 49.7 %collective-permute-start.43 = (f32[1,8,16]{2,0,1:T(1,128)}, f32[1,8,16]{2,0,1:T(1,128)}, u32[]{:S(2)}, u32[]{:S(2)}) collective-permute-start(f32[1,8,16]{2,0,1:T(1,128)} %get-tuple-element.224), channel_id=1, source_target_pairs={{4,0},{8,4},{12,8},{16,12},{20,16},{24,20},{28,24},{0,28},{5,1},{9... | collective-permute-start | bytes 1544 | tf_op jit(solution)/shard_map/ppermute | solution.py:23
  134.6 5.3 %collective-permute-start.29 = (f32[18,1,64]{2,1,0:T(1,128)S(1)}, f32[18,1,64]{2,1,0:T(1,128)S(1)}, u32[]{:S(2)}, u32[]{:S(2)}) collective-permute-start(f32[18,1,64]{2,1,0:T(1,128)S(1)} %get-tuple-element.178), channel_id=1, source_target_pairs={{1,0},{2,1},{3,2},{0,3},{5,4},{6,5},{7,6},{4,7},{9,8},{10,9},{11,1... | collective-permute-start | bytes 13832 | tf_op jit(solution)/shard_map/ppermute | solution.py:23
  137.0 7.6 %collective-permute-start.32 = (f32[10,1,32]{2,1,0:T(1,128)}, f32[10,1,32]{2,1,0:T(1,128)}, u32[]{:S(2)}, u32[]{:S(2)}) collective-permute-start(f32[10,1,32]{2,1,0:T(1,128)} %get-tuple-element.212), channel_id=1, source_target_pairs={{0,1},{1,2},{2,3},{3,0},{4,5},{5,6},{6,7},{7,4},{8,9},{9,10},{10,1... | collective-permute-start | bytes 3848 | tf_op jit(solution)/shard_map/ppermute | solution.py:22
  138.5 6.1 %collective-permute-start.33 = (f32[10,1,32]{2,1,0:T(1,128)}, f32[10,1,32]{2,1,0:T(1,128)}, u32[]{:S(2)}, u32[]{:S(2)}) collective-permute-start(f32[10,1,32]{2,1,0:T(1,128)} %get-tuple-element.211), channel_id=1, source_target_pairs={{1,0},{2,1},{3,2},{0,3},{5,4},{6,5},{7,6},{4,7},{9,8},{10,9},{11,1... | collective-permute-start | bytes 3848 | tf_op jit(solution)/shard_map/ppermute | solution.py:23
  (100 other events, 1705.0 us)
where the time goes:
time: 325 us; the launch traced here: 323 us
  starting transfers between devices  158 us (49%)
  waiting for transfers between devices  58 us (18%)
  local copies, waits for them, and re-layouts  48.8 us (15%)
  other arithmetic  40.9 us (13%)
  blocking collectives  16.3 us (5%)
    ppermute x48, starting transfers between devices, padded_2(): after = lax.ppermute(first, axis, down)  135 us
    ppermute x48, waiting for transfers between devices, padded_2(): before = lax.ppermute(last, axis, up)  49.6 us
    reshape x4, local copies, waits for them, and re-layouts, coarsen(): field.reshape(size_x // 2, 2, size_y // 2, 2, size_z // 2, 2)  40.2 us
    ppermute x48, starting transfers between devices, padded_2(): before = lax.ppermute(last, axis, up)  22.9 us
    reduce_sum x6, other arithmetic, coarsen(): field.reshape(size_x // 2, 2, size_y // 2, 2, size_z // 2, 2)  15.3 us
    add x25, other arithmetic, jacobi_sweep(): pressure + OMEGA * (right_side - apply_operator(padder(pressure), pressur...  11.6 us
    all_gather x1, blocking collectives, on_device(): lax.all_gather(coarse_perm, 'col', axis=1, tiled=True)  8.67 us
    ppermute x48, waiting for transfers between devices, padded_2(): after = lax.ppermute(first, axis, down)  8.41 us
  transfers between devices with their start and end apart: 96, of which 62 were waited for; matrix products, arithmetic and copies ran while one was open for 24% of the time, Pallas kernels for 0%

commit v1 on v0

v1 whole, which is shorter than its diff:
```python
import functools

import jax
import jax.numpy as jnp
from jax import lax
from jax.experimental import pallas as pl
from jax.experimental.pallas import tpu as pltpu
from jax.sharding import PartitionSpec as P

MESH = pl.DeviceIdType.MESH
OMEGA = 0.8
CSWEEPS = 16
PAD = 4


def lane_ids(rows):
    return lax.broadcasted_iota(jnp.int32, (rows, 128), 1)


def row_ids(rows):
    return lax.broadcasted_iota(jnp.int32, (rows, 128), 0)


def roll(value, shift, axis):
    return pltpu.roll(value, shift % value.shape[axis], axis)


def harmonic(left, right, scale):
    return (2.0 * scale) * left * right / (left + right)


def pair_sum(value, step):
    low = (lane_ids(value.shape[0]) // step) % 2 == 0
    return value + jnp.where(low, roll(value, -step, 1), roll(value, step, 1))


class Window:
    def __init__(self, nx, ny, step, scale):
        self.nx, self.ny, self.sub, self.step, self.scale = nx, ny, ny + 2 * PAD, step, scale

    def at(self, x):
        start = x * self.sub
        if not isinstance(x, int):
            start = pl.multiple_of(start, 8)
        return pl.ds(start, self.sub)

    def faces(self, perm, cx, cy, cz, diag, weight, lo, hi):
        lane = lane_ids(self.sub)

        def west(x, carry):
            cx[self.at(x), :] = harmonic(perm[self.at(x - 1), :], perm[self.at(x), :], self.scale)
            return carry

        lax.fori_loop(lo, hi + 1, west, 0)

        def cell(x, carry):
            k = perm[self.at(x), :]
            south = harmonic(roll(k, 1, 0), k, self.scale)
            under = jnp.where(lane < self.step, 0.0, harmonic(roll(k, self.step, 1), k, self.scale))
            outer = 2.0 * k * self.scale
            below = jnp.where(lane < self.step, outer, under)
            above = jnp.where(lane >= 128 - self.step, outer, roll(under, -self.step, 1))
            total = cx[self.at(x), :] + cx[self.at(x + 1), :] + south + roll(south, -1, 0)
            total = total + below + above
            cy[self.at(x), :] = south
            cz[self.at(x), :] = under
            diag[self.at(x), :] = total
            weight[self.at(x), :] = OMEGA / total
            return carry

        lax.fori_loop(lo, hi, cell, 0)

    def beside(self, x, v, cx, cy, cz):
        own = v[self.at(x), :]
        south, under = cy[self.at(x), :], cz[self.at(x), :]
        total = cx[self.at(x), :] * v[self.at(x - 1), :] + cx[self.at(x + 1), :] * v[self.at(x + 1), :]
        total = total + (south * roll(own, 1, 0) + roll(south * own, -1, 0))
        total = total + (under * roll(own, self.step, 1) + roll(under * own, -self.step, 1))
        return own, total

    def sweep(self, v, rhs, faces, lo, hi, store):
        cx, cy, cz, _, weight = faces

        def body(x, carry):
            own, total = self.beside(x, v, cx, cy, cz)
            store(x, (1.0 - OMEGA) * own + weight[self.at(x), :] * (rhs[self.at(x), :] + total))
            return carry

        lax.fori_loop(lo, hi, body, 0, unroll=2)

    def residual(self, x, v, rhs, faces):
        cx, cy, cz, diag, _ = faces
        own, total = self.beside(x, v, cx, cy, cz)
        return rhs[self.at(x), :] - diag[self.at(x), :] * own + total


class Packed:
    def __init__(self, rows, cols, level):
        self.rows, self.cols, self.level = rows, cols, level
        self.sub = cols * 8
        self.scale = 0.25**level
        self.ystep, self.zstep = (2, 4) if level == 2 else (4, 8)

    def at(self, r):
        return pl.ds(pl.multiple_of(r * self.sub, 8), self.sub)

    def prev(self, r):
        return lax.rem(r + self.rows - 1, self.rows)

    def next(self, r):
        return lax.rem(r + 1, self.rows)

    def west(self, here, before):
        j = lane_ids(self.sub) % 4
        if self.level == 3:
            return jnp.where(j > 0, roll(here, 1, 1), roll(before, -3, 1))
        odd = row_ids(self.sub) % 2 == 1
        up, up_before = roll(here, -1, 0), roll(before, -1, 0)
        other = jnp.where(j > 0, roll(up, 1, 1), roll(up_before, -3, 1))
        return jnp.where(odd, roll(here, 1, 0), other)

    def east(self, here, after):
        j = lane_ids(self.sub) % 4
        if self.level == 3:
            return jnp.where(j < 3, roll(here, -1, 1), roll(after, 3, 1))
        odd = row_ids(self.sub) % 2 == 1
        down, down_after = roll(here, 1, 0), roll(after, 1, 0)
        other = jnp.where(j < 3, roll(down, -1, 1), roll(down_after, 3, 1))
        return jnp.where(odd, other, roll(here, -1, 0))

    def loop(self, body):
        def step(r, carry):
            body(r)
            return carry

        lax.fori_loop(0, self.rows, step, 0, unroll=2)

    def faces(self, perm, cx, cy, cz, diag, weight):
        lane = lane_ids(self.sub)

        def first(r):
            k = perm[self.at(r), :]
            cx[self.at(r), :] = harmonic(self.west(k, perm[self.at(self.prev(r)), :]), k, self.scale)

        self.loop(first)

        def second(r):
            k = perm[self.at(r), :]
            lower = cx[self.at(r), :]
            south = harmonic(roll(k, self.ystep, 0), k, self.scale)
            under = harmonic(roll(k, self.zstep, 1), k, self.scale)
            under = jnp.where(lane < self.zstep, 0.0, under)
            outer = 2.0 * k * self.scale
            below = jnp.where(lane < self.zstep, outer, under)
            above = jnp.where(lane >= 128 - self.zstep, outer, roll(under, -self.zstep, 1))
            total = lower + self.east(lower, cx[self.at(self.next(r)), :])
            total = total + south + roll(south, -self.ystep, 0) + below + above
            cy[self.at(r), :] = south
            cz[self.at(r), :] = under
            diag[self.at(r), :] = total
            weight[self.at(r), :] = OMEGA / total

        self.loop(second)

    def beside(self, r, v, cx, cy, cz):
        own = v[self.at(r), :]
        lower, south, under = cx[self.at(r), :], cy[self.at(r), :], cz[self.at(r), :]
        before, after = self.at(self.prev(r)), self.at(self.next(r))
        total = lower * self.west(own, v[before, :])
        total = total + self.east(lower * own, cx[after, :] * v[after, :])
        total = total + (south * roll(own, self.ystep, 0) + roll(south * own, -self.ystep, 0))
        total = total + (under * roll(own, self.zstep, 1) + roll(under * own, -self.zstep, 1))
        return own, total

    def start(self, v, rhs, weight):
        def body(r):
            v[self.at(r), :] = weight[self.at(r), :] * rhs[self.at(r), :]

        self.loop(body)

    def sweep(self, v, new, rhs, faces):
        cx, cy, cz, _, weight = faces

        def body(r):
            own, total = self.beside(r, v, cx, cy, cz)
            update = weight[self.at(r), :] * (rhs[self.at(r), :] + total)
            new[self.at(r), :] = (1.0 - OMEGA) * own + update

        self.loop(body)

    def block_mean(self, value):
        row = row_ids(self.sub)
        value = value + jnp.where(row % 2 == 0, roll(value, -1, 0), roll(value, 1, 0))
        value = value + jnp.where(row // 2 % 2 == 0, roll(value, -2, 0), roll(value, 2, 0))
        return pair_sum(value, 4) * 0.125


class Exchange:
    def __init__(self, win, items, bufs, sems, base, ids):
        self.win, self.items, self.ids = win, items, ids
        self.ystage, self.yland, self.cstage, self.cland = bufs
        self.sems, self.base = sems, base
        self.layers = sum(h for _, h in items)

    def remote(self, src, dst, to):
        send, recv = self.sems
        copy = pltpu.make_async_remote_copy(
            src_ref=src, dst_ref=dst, send_sem=send.at[self.base], recv_sem=recv.at[self.base],
            device_id=to, device_id_type=MESH)
        self.base += 1
        copy.start()
        return copy

    def edge(self, h, side, i):
        ny, sub = self.win.ny, self.win.sub
        return (i, ny + i) if side == 0 else (ny - h + i, sub - h + i)

    def spans(self, h):
        return (PAD - h, PAD + self.win.nx)

    def start(self):
        (me_r, me_c), (left, right), (down, up) = self.ids
        nx, sub = self.win.nx, self.win.sub
        self.x_copies = []
        for ref, h in self.items:
            rows = h * sub
            lower, upper = PAD * sub, (PAD + nx - h) * sub
            self.x_copies.append(self.remote(
                ref.at[pl.ds(lower, rows), :], ref.at[pl.ds((PAD + nx) * sub, rows), :], (left, me_c)))
            self.x_copies.append(self.remote(
                ref.at[pl.ds(upper, rows), :], ref.at[pl.ds((PAD - h) * sub, rows), :], (right, me_c)))
        self.y_copies = []
        for side, to in ((0, down), (1, up)):
            n = 0
            for ref, h in self.items:
                for i in range(h):
                    mine, _ = self.edge(h, side, i)
                    self.ystage[side, n * nx:(n + 1) * nx, :] = ref[pl.ds(PAD * sub + mine, nx, stride=sub), :]
                    n += 1
            self.y_copies.append(self.remote(self.ystage.at[side], self.yland.at[side], (me_r, to)))

    def corners(self):
        (me_r, me_c), _, (down, up) = self.ids
        sub = self.win.sub
        for copy in self.x_copies:
            copy.wait()
        self.c_copies = []
        for side, to in ((0, down), (1, up)):
            n = 0
            for ref, h in self.items:
                for i in range(h):
                    mine, _ = self.edge(h, side, i)
                    for first in self.spans(h):
                        for x in range(first, first + h):
                            self.cstage[side, n:n + 1, :] = ref[pl.ds(x * sub + mine, 1), :]
                            n += 1
            self.c_copies.append(self.remote(self.cstage.at[side], self.cland.at[side], (me_r, to)))

    def finish(self):
        nx, sub = self.win.nx, self.win.sub
        for copy in self.y_copies:
            copy.wait()
        for copy in self.c_copies:
            copy.wait()
        for side in (0, 1):
            n, m = 0, 0
            for ref, h in self.items:
                for i in range(h):
                    _, halo = self.edge(h, side, i)
                    ref[pl.ds(PAD * sub + halo, nx, stride=sub), :] = self.yland[side, n * nx:(n + 1) * nx, :]
                    n += 1
                    for first in self.spans(h):
                        for x in range(first, first + h):
                            ref[pl.ds(x * sub + halo, 1), :] = self.cland[side, m:m + 1, :]
                            m += 1


def stage_sizes(win, halos):
    layers = sum(halos)
    corner = sum(2 * h * h for h in halos)
    corner = (corner + 7) // 8 * 8
    return [(2, layers * win.nx, 128)] * 2 + [(2, corner, 128)] * 2


def gather(src, land, tiles, sems, sizes, ids):
    rows, cols = sizes
    (me_r, me_c), _, _ = ids
    send, recv = sems

    def one(k, carry):
        to = (lax.rem(me_r + rows - k // cols, rows), lax.rem(me_c + cols - k % cols, cols))
        pltpu.make_async_remote_copy(
            src_ref=src, dst_ref=land.at[pl.ds(pl.multiple_of(k * 8, 8), 8), :], send_sem=send,
            recv_sem=recv, device_id=to, device_id_type=MESH).start()
        return carry

    lax.fori_loop(1, tiles, one, 0)


def gather_wait(land, tiles, sems, ids):
    (me_r, me_c), (left, _), _ = ids
    span = land.at[pl.ds(8, (tiles - 1) * 8), :]
    done = pltpu.make_async_remote_copy(
        src_ref=span, dst_ref=span, send_sem=sems[0], recv_sem=sems[1],
        device_id=(left, me_c), device_id_type=MESH)
    done.wait_send()
    done.wait_recv()


def cycle_kernel(sizes, wins, p_in, s_in, k_in, out, *scratch):
    rows, cols = sizes
    tiles = rows * cols
    fine, mid = wins
    scratch = list(scratch)

    def take(count):
        got, scratch[:count] = scratch[:count], []
        return got

    pw, pa, pb, sw, kw, vw = take(6)
    faces0 = take(5)
    b1, k1, va, vb, v1 = take(5)
    faces1 = take(5)
    k2, b2, p2a, p2b = take(4)
    faces2 = take(5)
    b3, p3a, p3b = take(3)
    faces3 = take(5)
    tmp, tile_b, tile_k = take(3)
    x0, x1, x2, x3 = take(4), take(4), take(4), take(4)
    send, recv, gsend, grecv = take(4)

    me_r, me_c = lax.axis_index("row"), lax.axis_index("col")
    ids = ((me_r, me_c),
           (lax.rem(me_r + rows - 1, rows), lax.rem(me_r + 1, rows)),
           (lax.rem(me_c + cols - 1, cols), lax.rem(me_c + 1, cols)))

    barrier = pltpu.get_barrier_semaphore()

    def greet(k, carry):
        to = (lax.rem(me_r + k // cols, rows), lax.rem(me_c + k % cols, cols))
        pl.semaphore_signal(barrier, inc=1, device_id=to, device_id_type=MESH)
        return carry

    lax.fori_loop(1, tiles, greet, 0)

    nx, ny, sub = fine.nx, fine.ny, fine.sub

    def bring(x, carry):
        at = pl.ds(pl.multiple_of((x + PAD) * sub, 8), ny)
        kw[at, :] = k_in[x]
        pw[at, :] = p_in[x]
        sw[at, :] = s_in[x]
        return carry

    lax.fori_loop(0, nx, bring, 0, unroll=2)
    pl.semaphore_wait(barrier, tiles - 1)

    first = Exchange(fine, [(kw, 3), (pw, 3), (sw, 2)], x0, (send, recv), 0, ids)
    first.start()

    def k_mean(i, carry):
        x = 2 * i
        total = pair_sum(k_in[x] + k_in[x + 1], 1)
        tmp[0:ny, :] = total
        halves = tmp[pl.ds(0, ny // 2, stride=2), :] + tmp[pl.ds(1, ny // 2, stride=2), :]
        k1[pl.ds(pl.multiple_of((i + PAD) * mid.sub, 8), mid.ny), :] = halves * 0.125
        return carry

    lax.fori_loop(0, nx // 2, k_mean, 0)
    first.corners()

    def to_tile(row_of, tile):
        lane = lane_ids(mid.ny // 2)
        packs = [None, None]
        for x in range(mid.nx // 2):
            j, i = x // 2, x % 2
            total = pair_sum(row_of(2 * x + PAD) + row_of(2 * x + 1 + PAD), 2)
            tmp[0:mid.sub, :] = total
            n = mid.ny // 2
            block = (tmp[pl.ds(0, n, stride=2), :] + tmp[pl.ds(1, n, stride=2), :]) * 0.125
            packs[i] = block if j == 0 else jnp.where(lane % 4 == j, block, packs[i])
        for i in range(2):
            tile[pl.ds(i, mid.ny // 2, stride=2), :] = packs[i]

    to_tile(lambda x: k1[mid.at(x), :], tile_k)
    k2[0:8, :] = tile_k[...]
    gather(tile_k, k2, tiles, (gsend.at[0], grecv.at[0]), sizes, ids)

    first.finish()
    second = Exchange(mid, [(k1, 3)], x1, (send, recv), first.base, ids)
    second.start()

    lo, hi = PAD, PAD + nx
    fine.faces(kw, *faces0, lo - 2, hi + 2)

    def put(win, ref):
        def store(x, value):
            ref[win.at(x), :] = value
        return store

    def put_both(x, value):
        pb[fine.at(x), :] = value

    fine.sweep(pw, sw, faces0, lo - 2, hi + 2, put(fine, pa))
    fine.sweep(pa, sw, faces0, lo - 1, hi + 1, put_both)

    def restrict0(i, carry):
        x = 2 * i + PAD
        total = fine.residual(x, pb, sw, faces0) + fine.residual(x + 1, pb, sw, faces0)
        tmp[0:sub, :] = pair_sum(total, 1)
        halves = tmp[pl.ds(0, ny // 2, stride=2), :] + tmp[pl.ds(1, ny // 2, stride=2), :]
        b1[pl.ds(pl.multiple_of((i + PAD) * mid.sub, 8), mid.ny), :] = halves * 0.125
        return carry

    lax.fori_loop(0, nx // 2, restrict0, 0)
    second.corners()

    third = Exchange(mid, [(b1, 2)], x2, (send, recv), second.base, ids)
    third.start()

    def keep0(x, carry):
        vw[fine.at(x), :] = pb[fine.at(x), :]
        return carry

    lax.fori_loop(lo, hi, keep0, 0, unroll=2)
    second.finish()
    lo1, hi1 = PAD, PAD + mid.nx
    mid.faces(k1, *faces1, lo1 - 2, hi1 + 2)
    third.corners()
    third.finish()

    def zero_sweep(x, carry):
        va[mid.at(x), :] = faces1[4][mid.at(x), :] * b1[mid.at(x), :]
        return carry

    lax.fori_loop(lo1 - 2, hi1 + 2, zero_sweep, 0)
    mid.sweep(va, b1, faces1, lo1 - 1, hi1 + 1, put(mid, vb))
    to_tile(lambda x: mid.residual(x, vb, b1, faces1), tile_b)
    b2[0:8, :] = tile_b[...]
    gather(tile_b, b2, tiles, (gsend.at[1], grecv.at[1]), sizes, ids)

    def keep1(x, carry):
        v1[mid.at(x), :] = vb[mid.at(x), :]
        return carry

    lax.fori_loop(lo1, hi1, keep1, 0)
    fourth = Exchange(mid, [(v1, 3)], x3[:4], (send, recv), third.base, ids)
    fourth.start()
    fifth = Exchange(fine, [(vw, 2)], take(4), (send, recv), fourth.base + 2, ids)
    fifth.start()

    coarse2, coarse3 = Packed(rows, cols, 2), Packed(rows, cols, 3)
    gather_wait(k2, tiles, (gsend.at[0], grecv.at[0]), ids)
    coarse2.faces(k2, *faces2)

    def k_coarsest(r):
        b3[coarse3.at(r), :] = coarse2.block_mean(k2[coarse2.at(r), :])

    coarse3.loop(k_coarsest)
    coarse3.faces(b3, *faces3)
    fourth.corners()
    fifth.corners()

    gather_wait(b2, tiles, (gsend.at[1], grecv.at[1]), ids)
    coarse2.start(p2a, b2, faces2[4])
    coarse2.sweep(p2a, p2b, b2, faces2)

    def restrict2(r):
        own, total = coarse2.beside(r, p2b, *faces2[:3])
        left = b2[coarse2.at(r), :] - faces2[3][coarse2.at(r), :] * own + total
        b3[coarse3.at(r), :] = coarse2.block_mean(left)

    coarse2.loop(restrict2)
    coarse3.start(p3a, b3, faces3[4])

    def two(i, carry):
        coarse3.sweep(p3a, p3b, b3, faces3)
        coarse3.sweep(p3b, p3a, b3, faces3)
        return carry

    lax.fori_loop(0, (CSWEEPS - 1) // 2, two, 0)
    coarse3.sweep(p3a, p3b, b3, faces3)

    def correct2(r):
        p2a[coarse2.at(r), :] = p2b[coarse2.at(r), :] + p3b[coarse3.at(r), :]

    coarse2.loop(correct2)
    coarse2.sweep(p2a, p2b, b2, faces2)
    coarse2.sweep(p2b, p2a, b2, faces2)

    fourth.finish()
    span = coarse2.sub
    lane = lane_ids(span)
    for dr, j in ((-1, 3), (0, 0), (0, 1), (0, 2), (0, 3), (1, 0)):
        part = p2a[(dr % rows) * span:(dr % rows + 1) * span, :]
        part = pair_sum(pair_sum(jnp.where(lane % 4 == j, part, 0.0), 1), 2)
        wrapped = roll(part, 16 - span, 0)
        tmp[0:16, :] = jnp.where(row_ids(16) < 12, part[0:16, :], wrapped[0:16, :])
        for i in range(2):
            e = tmp[pl.ds(i, 8, stride=2), :]
            x = 2 * (8 * dr + 2 * j + i) + PAD
            for row in (x, x + 1):
                for half in range(2):
                    at = pl.ds(row * mid.sub + half, 8, stride=2)
                    va[at, :] = v1[at, :] + e
    mid.sweep(va, b1, faces1, lo1 - 2, hi1 + 2, put(mid, vb))
    mid.sweep(vb, b1, faces1, lo1 - 1, hi1 + 1, put(mid, va))

    fifth.finish()

    def correct0(r, carry):
        base = pl.multiple_of(r * mid.sub, 8)
        upper = va[pl.ds(base, mid.sub), :]
        own, low = upper[0:8, :], upper[8:16, :]
        for half in range(2):
            tmp[pl.ds(half, 8, stride=2), :] = own
            tmp[pl.ds(16 + half, 2, stride=2), :] = low[0:2, :]
            tmp[pl.ds(20 + half, 2, stride=2), :] = low[6:8, :]
        e = tmp[0:sub, :]
        for x in (2 * r - PAD, 2 * r - PAD + 1):
            pa[fine.at(x), :] = vw[fine.at(x), :] + e
        return carry

    lax.fori_loop(lo1 - 1, hi1 + 1, correct0, 0)
    fine.sweep(pa, sw, faces0, lo - 1, hi + 1, put(fine, pb))

    def give(x, value):
        out[x - PAD] = value[0:ny, :]

    fine.sweep(pb, sw, faces0, lo, hi, give)


def on_device(sizes, pressure_in, source, permeability):
    rows, cols = sizes
    nx, ny, _ = pressure_in.shape
    fine, mid = Window(nx, ny, 1, 1.0), Window(nx // 2, ny // 2, 2, 0.25)

    def window(win):
        return pltpu.VMEM(((win.nx + 2 * PAD) * win.sub, 128), jnp.float32)

    packed = pltpu.VMEM((rows * cols * 8, 128), jnp.float32)
    scratch = [window(fine)] * 11 + [window(mid)] * 10 + [packed] * 17
    scratch += [pltpu.VMEM((32, 128), jnp.float32)] + [pltpu.VMEM((8, 128), jnp.float32)] * 2
    for win, halos in ((fine, (3, 3, 2)), (mid, (3,)), (mid, (2,)), (mid, (3,))):
        scratch += [pltpu.VMEM(size, jnp.float32) for size in stage_sizes(win, halos)]
    scratch += [pltpu.SemaphoreType.DMA((40,))] * 2 + [pltpu.SemaphoreType.DMA((2,))] * 2
    scratch += [pltpu.VMEM(size, jnp.float32) for size in stage_sizes(fine, (2,))]
    vmem = pl.BlockSpec(memory_space=pltpu.VMEM)
    return pl.pallas_call(
        functools.partial(cycle_kernel, sizes, (fine, mid)),
        out_shape=jax.ShapeDtypeStruct(pressure_in.shape, jnp.float32),
        in_specs=[vmem] * 3,
        out_specs=vmem,
        scratch_shapes=scratch,
        compiler_params=pltpu.CompilerParams(
            collective_id=0, has_side_effects=True, vmem_limit_bytes=58 * 1024 * 1024),
    )(pressure_in, source, permeability)


def solution(mesh):
    sizes = (mesh.shape["row"], mesh.shape["col"])
    placed = (P("row", "col", None), P("row", "col", None), P("row", "col", None))
    return jax.shard_map(
        functools.partial(on_device, sizes), mesh=mesh, in_specs=placed,
        out_specs=P("row", "col", None), check_vma=False)
```

time: 325 us -> 62.7 us (0.19)
  starting transfers between devices: 158 us -> 0 us
  Pallas kernels: 0 us -> 60.9 us
  waiting for transfers between devices: 58 us -> 0 us
  local copies, waits for them, and re-layouts: 48.8 us -> 1.67 us
  other arithmetic: 40.9 us -> 0 us
  blocking collectives: 16.3 us -> 0 us
    ppermute x96 -> x0, starting transfers between devices: 158 us -> none  [the longest x48 135 us: padded_2(): after = lax.ppermute(first, axis, down)]
    pallas_call x0 -> x1, Pallas kernels: none -> 60.9 us  [on_device(): pl.pallas_call(functools.partial(cycle_kernel, sizes, (fine, mid)), out_s...]
    ppermute x96 -> x0, waiting for transfers between devices: 58 us -> none  [the longest x48 49.6 us: padded_2(): before = lax.ppermute(last, axis, up)]
    reshape x10 -> x0, local copies, waits for them, and re-layouts: 41.2 us -> none  [the longest x4 40.2 us: coarsen(): field.reshape(size_x // 2, 2, size_y // 2, 2, size_z // 2, 2)]
    all_gather x2 -> x0, blocking collectives: 16.3 us -> none  [the longest x1 8.67 us: on_device(): lax.all_gather(coarse_perm, 'col', axis=1, tiled=True)]
    reduce_sum x6 -> x0, other arithmetic: 15.3 us -> none  [coarsen(): field.reshape(size_x // 2, 2, size_y // 2, 2, size_z // 2, 2)]
    add x28 -> x0, other arithmetic: 11.6 us -> none  [the longest x25 11.6 us: jacobi_sweep(): pressure + OMEGA * (right_side - apply_operator(padder(pressure), pressur...]
    mul x7 -> x0, other arithmetic: 6.25 us -> none  [the longest x4 3.97 us: coefficients(): above = jnp.concatenate([inner, 2.0 * center[:, :, -1:] * scale], axis=2)]
  transfers between devices with their start and end apart: 96 -> 0, of which waited for: 62 -> 0; matrix products, arithmetic and copies ran while one was open for 24% -> 0% of each run, Pallas kernels for 0% -> 0%
where the time goes in v1:
time: 62.7 us; the launch traced here: 62.6 us
  Pallas kernels  60.9 us (97%)
  local copies, waits for them, and re-layouts  1.67 us (3%)
    pallas_call x1, Pallas kernels, on_device(): pl.pallas_call(functools.partial(cycle_kernel, sizes, (fine, mid)), out_s...  60.9 us
    unnamed x1, local copies, waits for them, and re-layouts  1.67 us

profile of v1, /device:TPU:0, one launch (start us, length us, event | category | flops | bytes accessed | tf_op | source)
XLA Modules:
  0.0 62.6 jit_solution(93303885976439168)
XLA Ops:
  0.0 60.9 %shard_map.37 = f32[32,16,128]{2,1,0:T(8,128)} custom-call(f32[32,16,128]{2,1,0:T(8,128)} %p_in.1, f32[32,16,128]{2,1,0:T(8,128)} %s_in.1, f32[32,16,128]{2,1,0:T(8,128)} %k_in.1), custom_call_target="tpu_custom_call" | custom-call | tf_op jit(solution)/shard_map/pallas_call | solution.py:549
  60.9 1.7 %copy.5 = f32[32,16,128]{2,1,0:T(8,128)} copy(f32[32,16,128]{2,1,0:T(8,128)} %shard_map.37) | data formatting | bytes 524288

commit v2 on v0

v2 whole, which is shorter than its diff:
```python
import functools

import jax
import jax.numpy as jnp
from jax import lax
from jax.experimental import pallas as pl
from jax.experimental.pallas import tpu as pltpu
from jax.sharding import PartitionSpec as P

MESH = pl.DeviceIdType.MESH
OMEGA = 0.8
CSWEEPS = 16
PAD = 4


def lane_ids(rows):
    return lax.broadcasted_iota(jnp.int32, (rows, 128), 1)


def row_ids(rows):
    return lax.broadcasted_iota(jnp.int32, (rows, 128), 0)


def roll(value, shift, axis):
    return pltpu.roll(value, shift % value.shape[axis], axis)


def harmonic(left, right, scale):
    return (2.0 * scale) * left * right / (left + right)


def pair_sum(value, step):
    low = (lane_ids(value.shape[0]) // step) % 2 == 0
    return value + jnp.where(low, roll(value, -step, 1), roll(value, step, 1))


class Window:
    def __init__(self, nx, ny, step, scale):
        self.nx, self.ny, self.sub, self.step, self.scale = nx, ny, ny + 2 * PAD, step, scale

    def at(self, x):
        start = x * self.sub
        if not isinstance(x, int):
            start = pl.multiple_of(start, 8)
        return pl.ds(start, self.sub)

    def groups(self, lo, hi, most, body):
        count = -(-(hi - lo) // most)
        size = -(-(hi - lo) // count)

        def step(g, carry):
            start = jnp.minimum(lo + g * size, hi - size)
            body([start + i for i in range(size)])
            return carry

        lax.fori_loop(0, count, step, 0)

    def faces(self, perm, cx, cy, cz, diag, weight, lo, hi, most):
        lane = lane_ids(self.sub)

        def body(rows):
            ks = [perm[self.at(x), :] for x in [rows[0] - 1] + rows + [rows[-1] + 1]]
            west = [harmonic(k, other, self.scale) for k, other in zip(ks[:-1], ks[1:])]
            found = []
            for i, k in enumerate(ks[1:-1]):
                south = harmonic(roll(k, 1, 0), k, self.scale)
                under = harmonic(roll(k, self.step, 1), k, self.scale)
                under = jnp.where(lane < self.step, 0.0, under)
                outer = 2.0 * k * self.scale
                below = jnp.where(lane < self.step, outer, under)
                above = jnp.where(lane >= 128 - self.step, outer, roll(under, -self.step, 1))
                total = west[i] + west[i + 1] + south + roll(south, -1, 0) + below + above
                found.append((south, under, total, OMEGA / total))
            for x, lower, (south, under, total, inverse) in zip(rows, west, found):
                cx[self.at(x), :] = lower
                cy[self.at(x), :] = south
                cz[self.at(x), :] = under
                diag[self.at(x), :] = total
                weight[self.at(x), :] = inverse
            cx[self.at(rows[-1] + 1), :] = west[-1]

        self.groups(lo, hi, most, body)

    def beside(self, rows, v, cx, cy, cz):
        vs = [v[self.at(x), :] for x in [rows[0] - 1] + rows + [rows[-1] + 1]]
        west = [cx[self.at(x), :] for x in rows + [rows[-1] + 1]]
        out = []
        for i, x in enumerate(rows):
            own, south, under = vs[i + 1], cy[self.at(x), :], cz[self.at(x), :]
            total = west[i] * vs[i] + west[i + 1] * vs[i + 2]
            total = total + (south * roll(own, 1, 0) + roll(south * own, -1, 0))
            total = total + (under * roll(own, self.step, 1) + roll(under * own, -self.step, 1))
            out.append((own, total))
        return out

    def sweep(self, v, rhs, faces, lo, hi, most, store):
        cx, cy, cz, _, weight = faces

        def body(rows):
            new = [(1.0 - OMEGA) * own + weight[self.at(x), :] * (rhs[self.at(x), :] + total)
                   for x, (own, total) in zip(rows, self.beside(rows, v, cx, cy, cz))]
            for x, value in zip(rows, new):
                store(x, value)

        self.groups(lo, hi, most, body)

    def residual(self, rows, v, rhs, faces):
        cx, cy, cz, diag, _ = faces
        return [rhs[self.at(x), :] - diag[self.at(x), :] * own + total
                for x, (own, total) in zip(rows, self.beside(rows, v, cx, cy, cz))]


class Packed:
    def __init__(self, rows, cols):
        self.rows, self.cols, self.sub = rows, cols, cols * 8
        self.scale = 0.25**2

    def at(self, r):
        return pl.ds(pl.multiple_of(r * self.sub, 8), self.sub)

    def west(self, here, before):
        j = lane_ids(self.sub) % 4
        odd = row_ids(self.sub) % 2 == 1
        up, up_before = roll(here, -1, 0), roll(before, -1, 0)
        other = jnp.where(j > 0, roll(up, 1, 1), roll(up_before, -3, 1))
        return jnp.where(odd, roll(here, 1, 0), other)

    def east(self, here, after):
        j = lane_ids(self.sub) % 4
        odd = row_ids(self.sub) % 2 == 1
        down, down_after = roll(here, 1, 0), roll(after, 1, 0)
        other = jnp.where(j < 3, roll(down, -1, 1), roll(down_after, 3, 1))
        return jnp.where(odd, other, roll(here, -1, 0))

    def groups(self, body):
        size = 4 if self.rows % 4 == 0 else 1

        def step(g, carry):
            body([g * size + i for i in range(size)])
            return carry

        lax.fori_loop(0, self.rows // size, step, 0)

    def around(self, rows):
        return [lax.rem(rows[0] + self.rows - 1, self.rows)] + rows + [lax.rem(rows[-1] + 1, self.rows)]

    def faces(self, perm, cx, cy, cz, diag, weight):
        lane = lane_ids(self.sub)

        def first(rows):
            ks = [perm[self.at(r), :] for r in self.around(rows)]
            new = [harmonic(self.west(k, before), k, self.scale) for before, k in zip(ks, ks[1:-1])]
            for r, value in zip(rows, new):
                cx[self.at(r), :] = value

        self.groups(first)

        def second(rows):
            west = [cx[self.at(r), :] for r in self.around(rows)]
            found = []
            for i, r in enumerate(rows):
                k = perm[self.at(r), :]
                south = harmonic(roll(k, 2, 0), k, self.scale)
                under = jnp.where(lane < 4, 0.0, harmonic(roll(k, 4, 1), k, self.scale))
                outer = 2.0 * k * self.scale
                below = jnp.where(lane < 4, outer, under)
                above = jnp.where(lane >= 124, outer, roll(under, -4, 1))
                total = west[i + 1] + self.east(west[i + 1], west[i + 2])
                total = total + south + roll(south, -2, 0) + below + above
                found.append((south, under, total, OMEGA / total))
            for r, (south, under, total, inverse) in zip(rows, found):
                cy[self.at(r), :] = south
                cz[self.at(r), :] = under
                diag[self.at(r), :] = total
                weight[self.at(r), :] = inverse

        self.groups(second)

    def beside(self, rows, v, cx, cy, cz):
        vs = [v[self.at(r), :] for r in self.around(rows)]
        west = [cx[self.at(r), :] for r in self.around(rows)]
        flow = [c * value for c, value in zip(west[1:], vs[1:])]
        out = []
        for i, r in enumerate(rows):
            own, south, under = vs[i + 1], cy[self.at(r), :], cz[self.at(r), :]
            total = west[i + 1] * self.west(own, vs[i]) + self.east(flow[i], flow[i + 1])
            total = total + (south * roll(own, 2, 0) + roll(south * own, -2, 0))
            total = total + (under * roll(own, 4, 1) + roll(under * own, -4, 1))
            out.append((own, total))
        return out

    def start(self, v, rhs, weight):
        def body(rows):
            new = [weight[self.at(r), :] * rhs[self.at(r), :] for r in rows]
            for r, value in zip(rows, new):
                v[self.at(r), :] = value

        self.groups(body)

    def sweep(self, v, new, rhs, faces):
        cx, cy, cz, _, weight = faces

        def body(rows):
            values = [(1.0 - OMEGA) * own + weight[self.at(r), :] * (rhs[self.at(r), :] + total)
                      for r, (own, total) in zip(rows, self.beside(rows, v, cx, cy, cz))]
            for r, value in zip(rows, values):
                new[self.at(r), :] = value

        self.groups(body)

    def block_mean(self, value):
        row = row_ids(self.sub)
        value = value + jnp.where(row % 2 == 0, roll(value, -1, 0), roll(value, 1, 0))
        value = value + jnp.where(row // 2 % 2 == 0, roll(value, -2, 0), roll(value, 2, 0))
        return pair_sum(value, 4) * 0.125


class Coarsest:
    def __init__(self, rows, cols):
        self.g, self.q, self.sub = rows // 2, cols // 4, cols * 8
        self.cells = [(g, q) for g in range(self.g) for q in range(self.q)]
        self.scale = 0.25**3

    def at(self, r, c):
        return pl.ds(r * self.sub + c * 8, 8)

    def pack(self, ref):
        sublane, lane = row_ids(8) % 4, lane_ids(8) // 4 % 2
        out = {}
        for g, q in self.cells:
            halves = []
            for r in (2 * g, 2 * g + 1):
                half = ref[self.at(r, 4 * q), :]
                for c in (1, 2, 3):
                    half = jnp.where(sublane == c, ref[self.at(r, 4 * q + c), :], half)
                halves.append(half)
            out[g, q] = jnp.where(lane == 0, halves[0], halves[1])
        return out

    def repeated(self, v, r, c):
        value = v[r // 2, c // 4]
        high = lane_ids(8) // 4 % 2
        value = jnp.where(high == r % 2, value, roll(value, 4 if r % 2 == 0 else -4, 1))
        row = row_ids(8)
        value = jnp.where(row % 4 == c % 4, value, 0.0)
        value = value + jnp.where(row % 2 == 0, roll(value, -1, 0), roll(value, 1, 0))
        return value + jnp.where(row // 2 % 2 == 0, roll(value, -2, 0), roll(value, 2, 0))

    def lower_x(self, v, g, q):
        here = lane_ids(8) % 8 > 0
        return jnp.where(here, roll(v[g, q], 1, 1), roll(v[(g - 1) % self.g, q], -7, 1))

    def upper_x(self, v, g, q):
        here = lane_ids(8) % 8 < 7
        return jnp.where(here, roll(v[g, q], -1, 1), roll(v[(g + 1) % self.g, q], 7, 1))

    def lower_y(self, v, g, q):
        row = row_ids(8)
        other = jnp.where(row == 0, roll(v[g, (q - 1) % self.q], 1, 0), roll(v[g, q], -3, 0))
        return jnp.where(row >= 4, roll(v[g, q], 4, 0), other)

    def upper_y(self, v, g, q):
        row = row_ids(8)
        other = jnp.where(row == 7, roll(v[g, (q + 1) % self.q], -1, 0), roll(v[g, q], 3, 0))
        return jnp.where(row < 4, roll(v[g, q], 4, 0), other)

    def faces(self, k):
        lane = lane_ids(8)
        cx = {i: harmonic(self.lower_x(k, *i), k[i], self.scale) for i in self.cells}
        cy = {i: harmonic(self.lower_y(k, *i), k[i], self.scale) for i in self.cells}
        out = {}
        for i in self.cells:
            under = jnp.where(lane < 8, 0.0, harmonic(roll(k[i], 8, 1), k[i], self.scale))
            over = jnp.where(lane >= 120, 0.0, roll(under, -8, 1))
            outer = 2.0 * k[i] * self.scale
            below, above = jnp.where(lane < 8, outer, under), jnp.where(lane >= 120, outer, over)
            east, north = self.upper_x(cx, *i), self.upper_y(cy, *i)
            total = cx[i] + east + cy[i] + north + below + above
            weight = OMEGA / total
            out[i] = [weight * c for c in (cx[i], east, cy[i], north, under, over)] + [weight]
        return out

    def solve(self, faces, rhs):
        start = {i: faces(i, 6) * rhs[i] for i in self.cells}

        def sweep(_, carry):
            v = dict(zip(self.cells, carry))
            new = []
            for i in self.cells:
                side_x = faces(i, 0) * self.lower_x(v, *i) + faces(i, 1) * self.upper_x(v, *i)
                side_y = faces(i, 2) * self.lower_y(v, *i) + faces(i, 3) * self.upper_y(v, *i)
                side_z = faces(i, 4) * roll(v[i], 8, 1) + faces(i, 5) * roll(v[i], -8, 1)
                new.append(((1.0 - OMEGA) * v[i] + start[i] + side_z) + (side_x + side_y))
            return tuple(new)

        done = lax.fori_loop(1, CSWEEPS, sweep, tuple(start[i] for i in self.cells))
        return dict(zip(self.cells, done))


class Exchange:
    def __init__(self, win, items, bufs, sems, base, ids):
        self.win, self.items, self.ids = win, items, ids
        self.ystage, self.yland, self.cstage, self.cland = bufs
        self.sems, self.base = sems, base
        self.layers = sum(h for _, h in items)

    def remote(self, src, dst, to):
        send, recv = self.sems
        copy = pltpu.make_async_remote_copy(
            src_ref=src, dst_ref=dst, send_sem=send.at[self.base], recv_sem=recv.at[self.base],
            device_id=to, device_id_type=MESH)
        self.base += 1
        copy.start()
        return copy

    def edge(self, h, side, i):
        ny, sub = self.win.ny, self.win.sub
        return (i, ny + i) if side == 0 else (ny - h + i, sub - h + i)

    def start(self):
        (me_r, me_c), near_r, near_c = self.ids
        nx, sub = self.win.nx, self.win.sub
        self.copies = []
        for side in (0, 1):
            n = 0
            for ref, h in self.items:
                for i in range(h):
                    mine, _ = self.edge(h, side, i)
                    self.ystage[side, n:n + nx, :] = ref[pl.ds(PAD * sub + mine, nx, stride=sub), :]
                    n += nx
            to = (me_r, near_c[side])
            self.copies.append(self.remote(self.ystage.at[side], self.yland.at[side], to))
        for ref, h in self.items:
            rows = h * sub
            for side, mine, theirs in ((0, PAD, PAD + nx), (1, PAD + nx - h, PAD - h)):
                self.copies.append(self.remote(
                    ref.at[pl.ds(mine * sub, rows), :], ref.at[pl.ds(theirs * sub, rows), :],
                    (near_r[side], me_c)))
        for xside in (0, 1):
            for side in (0, 1):
                n, slot = 0, 2 * xside + side
                for ref, h in self.items:
                    first = PAD if xside == 0 else PAD + nx - h
                    for i in range(h):
                        mine, _ = self.edge(h, side, i)
                        self.cstage[slot, n:n + h, :] = ref[pl.ds(first * sub + mine, h, stride=sub), :]
                        n += h
                to = (near_r[xside], near_c[side])
                self.copies.append(self.remote(self.cstage.at[slot], self.cland.at[slot], to))

    def finish(self):
        nx, sub = self.win.nx, self.win.sub
        for copy in self.copies:
            copy.wait()
        for side in (0, 1):
            n, m = 0, 0
            for ref, h in self.items:
                for i in range(h):
                    _, halo = self.edge(h, side, i)
                    ref[pl.ds(PAD * sub + halo, nx, stride=sub), :] = self.yland[side, n:n + nx, :]
                    n += nx
                    for xside, first in ((0, PAD + nx), (1, PAD - h)):
                        corner = self.cland[2 * xside + side, m:m + h, :]
                        ref[pl.ds(first * sub + halo, h, stride=sub), :] = corner
                    m += h


def stage_sizes(win, halos):
    layers = sum(halos)
    corner = sum(h * h for h in halos)
    corner = (corner + 7) // 8 * 8
    return [(2, layers * win.nx, 128)] * 2 + [(4, corner, 128)] * 2


def wrapped(value, size):
    return jnp.where(value >= size, value - size, value)


def others(sizes, ids, body):
    rows, cols = sizes
    me_r, me_c = ids[0]
    to_cols = [me_c] + [wrapped(me_c + cols - c, cols) for c in range(1, cols)]

    def row(r, carry):
        to_row = wrapped(me_r + rows - r, rows)
        for c in range(cols):
            body(r * cols + c, (to_row, to_cols[c]))
        return carry

    for c in range(1, cols):
        body(c, (me_r, to_cols[c]))
    lax.fori_loop(1, rows, row, 0, unroll=rows <= 8)


def gather(src, land, sems, sizes, ids):
    def one(slot, to):
        at = slot * 8 if isinstance(slot, int) else pl.multiple_of(slot * 8, 8)
        pltpu.make_async_remote_copy(
            src_ref=src, dst_ref=land.at[pl.ds(at, 8), :], send_sem=sems[0], recv_sem=sems[1],
            device_id=to, device_id_type=MESH).start()

    others(sizes, ids, one)


def gather_wait(land, tiles, sems, ids):
    (me_r, me_c), (left, _), _ = ids
    span = land.at[pl.ds(8, (tiles - 1) * 8), :]
    done = pltpu.make_async_remote_copy(
        src_ref=span, dst_ref=span, send_sem=sems[0], recv_sem=sems[1],
        device_id=(left, me_c), device_id_type=MESH)
    done.wait_send()
    done.wait_recv()


def cycle_kernel(sizes, wins, p_hbm, s_hbm, k_hbm, out, *scratch):
    rows, cols = sizes
    tiles = rows * cols
    fine, mid = wins
    scratch = list(scratch)

    def take(count):
        got, scratch[:count] = scratch[:count], []
        return got

    p_in, s_in, k_in, in_sems = take(4)
    pw, pa, pb, sw, kw, vw = take(6)
    faces0 = take(5)
    b1, k1, va, vb, v1 = take(5)
    faces1 = take(5)
    k2, b2, p2a, p2b, b3 = take(5)
    faces2 = take(5)
    faces3 = take(1)[0]
    tmp, tile_b, tile_k = take(3)
    send, recv, gsend, grecv = take(4)
    bufs = [take(4) for _ in range(6)]

    loads = []
    for i, (src, dst) in enumerate(((k_hbm, k_in), (p_hbm, p_in), (s_hbm, s_in))):
        loads.append(pltpu.make_async_copy(src, dst, in_sems.at[i]))
        loads[-1].start()

    me_r, me_c = lax.axis_index("row"), lax.axis_index("col")
    ids = ((me_r, me_c),
           (wrapped(me_r + rows - 1, rows), wrapped(me_r + 1, rows)),
           (wrapped(me_c + cols - 1, cols), wrapped(me_c + 1, cols)))

    barrier = pltpu.get_barrier_semaphore()
    others(sizes, ids, lambda _, to: pl.semaphore_signal(
        barrier, inc=1, device_id=to, device_id_type=MESH))

    nx, ny, sub = fine.nx, fine.ny, fine.sub

    def bring(pairs):
        def body(i, carry):
            for x in range(4):
                at = pl.ds(pl.multiple_of((4 * i + x + PAD) * sub, 8), ny)
                for src, dst in pairs:
                    dst[at, :] = src[4 * i + x]
            return carry

        lax.fori_loop(0, nx // 4, body, 0)

    base = 0

    def exchange(win, items, buf):
        nonlocal base
        made = Exchange(win, items, buf, (send, recv), base, ids)
        made.start()
        base = made.base
        return made

    loads[0].wait()
    bring([(k_in, kw)])
    loads[1].wait()
    loads[2].wait()
    bring([(p_in, pw), (s_in, sw)])
    pl.semaphore_wait(barrier, tiles - 1)
    halo_k = exchange(fine, [(kw, 3)], bufs[0])
    halo_p = exchange(fine, [(pw, 3), (sw, 2)], bufs[1])

    def halves(slot, value, n):
        at = slot * sub
        tmp[at:at + value.shape[0], :] = value
        return lambda: tmp[pl.ds(at, n, stride=2), :] + tmp[pl.ds(at + 1, n, stride=2), :]

    def to_mid(i, ref, sums):
        made = [halves(n, value, ny // 2) for n, value in enumerate(sums)]
        made = [value() * 0.125 for value in made]
        for n, value in enumerate(made):
            at = (i * len(sums) + n + PAD) * mid.sub
            ref[pl.ds(pl.multiple_of(at, 8), mid.ny), :] = value

    def k_mean(i, carry):
        to_mid(i, k1, [pair_sum(k_in[8 * i + 2 * n] + k_in[8 * i + 2 * n + 1], 1) for n in range(4)])
        return carry

    lax.fori_loop(0, nx // 8, k_mean, 0)

    def to_tile(values, tile):
        n = mid.ny // 2
        lane = lane_ids(n)
        made = [halves(x, pair_sum(values[2 * x] + values[2 * x + 1], 2), n) for x in range(mid.nx // 2)]
        made = [value() * 0.125 for value in made]
        for i in range(2):
            pack = made[i]
            for j in range(1, 4):
                pack = jnp.where(lane % 4 == j, made[2 * j + i], pack)
            tile[pl.ds(i, n, stride=2), :] = pack

    lo, hi, lo1, hi1 = PAD, PAD + nx, PAD, PAD + mid.nx
    to_tile([k1[mid.at(x), :] for x in range(lo1, hi1)], tile_k)
    k2[0:8, :] = tile_k[...]
    gather(tile_k, k2, (gsend.at[0], grecv.at[0]), sizes, ids)
    halo_k1 = exchange(mid, [(k1, 3)], bufs[2])

    halo_k.finish()
    fine.faces(kw, *faces0, lo - 2, hi + 2, 6)
    halo_p.finish()

    def put(win, ref):
        def store(x, value):
            ref[win.at(x), :] = value
        return store

    def put_both(x, value):
        pb[fine.at(x), :] = value

    fine.sweep(pw, sw, faces0, lo - 2, hi + 2, 9, put(fine, pa))
    fine.sweep(pa, sw, faces0, lo - 1, hi + 1, 9, put_both)

    def restrict0(i, carry):
        left = fine.residual([8 * i + PAD + n for n in range(8)], pb, sw, faces0)
        to_mid(i, b1, [pair_sum(left[2 * n] + left[2 * n + 1], 1) for n in range(4)])
        return carry

    lax.fori_loop(0, nx // 8, restrict0, 0)
    halo_b1 = exchange(mid, [(b1, 2)], bufs[3])

    def keep(win, src, dst):
        def body(i, carry):
            values = [src[win.at(4 * i + n + PAD), :] for n in range(4)]
            for n in range(4):
                dst[win.at(4 * i + n + PAD), :] = values[n]
            return carry

        lax.fori_loop(0, win.nx // 4, body, 0)

    keep(fine, pb, vw)
    halo_k1.finish()
    mid.faces(k1, *faces1, lo1 - 2, hi1 + 2, 10)
    coarse2, coarse3 = Packed(rows, cols), Coarsest(rows, cols)
    halo_b1.finish()

    def zero_sweep(xs):
        new = [faces1[4][mid.at(x), :] * b1[mid.at(x), :] for x in xs]
        for x, value in zip(xs, new):
            va[mid.at(x), :] = value

    mid.groups(lo1 - 2, hi1 + 2, 10, zero_sweep)
    mid.sweep(va, b1, faces1, lo1 - 1, hi1 + 1, 11, put(mid, vb))
    to_tile(mid.residual(list(range(lo1, hi1)), vb, b1, faces1), tile_b)
    b2[0:8, :] = tile_b[...]
    gather(tile_b, b2, (gsend.at[1], grecv.at[1]), sizes, ids)
    keep(mid, vb, v1)
    halo_v1 = exchange(mid, [(v1, 3)], bufs[4])
    halo_vw = exchange(fine, [(vw, 2)], bufs[5])

    gather_wait(k2, tiles, (gsend.at[0], grecv.at[0]), ids)
    coarse2.faces(k2, *faces2)

    def k_coarsest(rs):
        new = [coarse2.block_mean(k2[coarse2.at(r), :]) for r in rs]
        for r, value in zip(rs, new):
            b3[coarse2.at(r), :] = value

    coarse2.groups(k_coarsest)
    for n, group in enumerate(coarse3.faces(coarse3.pack(b3)).values()):
        for side, value in enumerate(group):
            faces3[n, side] = value

    gather_wait(b2, tiles, (gsend.at[1], grecv.at[1]), ids)
    coarse2.start(p2a, b2, faces2[4])
    coarse2.sweep(p2a, p2b, b2, faces2)

    def restrict2(rs):
        new = [coarse2.block_mean(b2[coarse2.at(r), :] - faces2[3][coarse2.at(r), :] * own + total)
               for r, (own, total) in zip(rs, coarse2.beside(rs, p2b, *faces2[:3]))]
        for r, value in zip(rs, new):
            b3[coarse2.at(r), :] = value

    coarse2.groups(restrict2)
    e3 = coarse3.solve(lambda i, side: faces3[coarse3.cells.index(i), side], coarse3.pack(b3))
    for r in range(rows):
        for c in range(cols):
            at = coarse3.at(r, c)
            p2a[at, :] = p2b[at, :] + coarse3.repeated(e3, r, c)
    coarse2.sweep(p2a, p2b, b2, faces2)
    coarse2.sweep(p2b, p2a, b2, faces2)

    halo_v1.finish()
    span = coarse2.sub
    lane = lane_ids(span)
    places = ((-1, 3), (0, 0), (0, 1), (0, 2), (0, 3), (1, 0))
    for n, (dr, j) in enumerate(places):
        part = p2a[(dr % rows) * span:(dr % rows + 1) * span, :]
        part = pair_sum(pair_sum(jnp.where(lane % 4 == j, part, 0.0), 1), 2)
        turned = roll(part, 16 - span, 0)
        tmp[16 * n:16 * n + 16, :] = jnp.where(row_ids(16) < 12, part[0:16, :], turned[0:16, :])
    for n, (dr, j) in enumerate(places):
        for i in range(2):
            e = tmp[pl.ds(16 * n + i, 8, stride=2), :]
            x = 2 * (8 * dr + 2 * j + i) + PAD
            for row in (x, x + 1):
                for half in range(2):
                    at = pl.ds(row * mid.sub + half, 8, stride=2)
                    va[at, :] = v1[at, :] + e
    mid.sweep(va, b1, faces1, lo1 - 2, hi1 + 2, 11, put(mid, vb))
    mid.sweep(vb, b1, faces1, lo1 - 1, hi1 + 1, 11, put(mid, va))

    halo_vw.finish()

    def correct0(g, carry):
        rs = [lo1 - 1 + 6 * g + n for n in range(6)]
        for n, r in enumerate(rs):
            e = va[mid.at(r), :]
            for half in range(2):
                tmp[pl.ds(n * sub + half, 8, stride=2), :] = e[0:8, :]
                tmp[pl.ds(n * sub + 16 + half, 2, stride=2), :] = e[8:10, :]
                tmp[pl.ds(n * sub + 20 + half, 2, stride=2), :] = e[14:16, :]
        new = []
        for n, r in enumerate(rs):
            e = tmp[n * sub:(n + 1) * sub, :]
            for x in (2 * r - PAD, 2 * r - PAD + 1):
                new.append((x, vw[fine.at(x), :] + e))
        for x, value in new:
            pa[fine.at(x), :] = value
        return carry

    lax.fori_loop(0, (mid.nx + 2) // 6, correct0, 0)
    fine.sweep(pa, sw, faces0, lo - 1, hi + 1, 9, put(fine, pb))

    def give(x, value):
        out[x - PAD] = value[0:ny, :]

    fine.sweep(pb, sw, faces0, lo, hi, 8, give)


def on_device(sizes, pressure_in, source, permeability):
    rows, cols = sizes
    nx, ny, _ = pressure_in.shape
    fine, mid = Window(nx, ny, 1, 1.0), Window(nx // 2, ny // 2, 2, 0.25)

    def window(win):
        return pltpu.VMEM(((win.nx + 2 * PAD) * win.sub, 128), jnp.float32)

    packed = pltpu.VMEM((rows * cols * 8, 128), jnp.float32)
    scratch = [pltpu.VMEM(pressure_in.shape, jnp.float32)] * 3 + [pltpu.SemaphoreType.DMA((3,))]
    scratch += [window(fine)] * 11 + [window(mid)] * 10 + [packed] * 10
    scratch += [pltpu.VMEM((rows * cols // 8, 7, 8, 128), jnp.float32)]
    scratch += [pltpu.VMEM((8 * fine.sub, 128), jnp.float32)] + [pltpu.VMEM((8, 128), jnp.float32)] * 2
    scratch += [pltpu.SemaphoreType.DMA((64,))] * 2 + [pltpu.SemaphoreType.DMA((2,))] * 2
    for win, halos in ((fine, (3,)), (fine, (3, 2)), (mid, (3,)), (mid, (2,)), (mid, (3,)), (fine, (2,))):
        scratch += [pltpu.VMEM(size, jnp.float32) for size in stage_sizes(win, halos)]
    anywhere = pl.BlockSpec(memory_space=pl.ANY)
    return pl.pallas_call(
        functools.partial(cycle_kernel, sizes, (fine, mid)),
        out_shape=jax.ShapeDtypeStruct(pressure_in.shape, jnp.float32),
        in_specs=[anywhere] * 3,
        out_specs=pl.BlockSpec(memory_space=pltpu.VMEM),
        scratch_shapes=scratch,
        compiler_params=pltpu.CompilerParams(
            collective_id=0, has_side_effects=True, vmem_limit_bytes=58 * 1024 * 1024),
    )(pressure_in, source, permeability)


def solution(mesh):
    sizes = (mesh.shape["row"], mesh.shape["col"])
    placed = (P("row", "col", None), P("row", "col", None), P("row", "col", None))
    return jax.shard_map(
        functools.partial(on_device, sizes), mesh=mesh, in_specs=placed,
        out_specs=P("row", "col", None), check_vma=False)
```

time: 325 us -> 38.2 us (0.12)
  starting transfers between devices: 158 us -> 0 us
  waiting for transfers between devices: 58 us -> 0 us
  local copies, waits for them, and re-layouts: 48.8 us -> 1.67 us
  other arithmetic: 40.9 us -> 0 us
  Pallas kernels: 0 us -> 36.3 us
  blocking collectives: 16.3 us -> 0 us
    ppermute x96 -> x0, starting transfers between devices: 158 us -> none  [the longest x48 135 us: padded_2(): after = lax.ppermute(first, axis, down)]
    ppermute x96 -> x0, waiting for transfers between devices: 58 us -> none  [the longest x48 49.6 us: padded_2(): before = lax.ppermute(last, axis, up)]
    reshape x10 -> x0, local copies, waits for them, and re-layouts: 41.2 us -> none  [the longest x4 40.2 us: coarsen(): field.reshape(size_x // 2, 2, size_y // 2, 2, size_z // 2, 2)]
    pallas_call x0 -> x1, Pallas kernels: none -> 36.3 us  [on_device(): pl.pallas_call(functools.partial(cycle_kernel, sizes, (fine, mid)), out_s...]
    all_gather x2 -> x0, blocking collectives: 16.3 us -> none  [the longest x1 8.67 us: on_device(): lax.all_gather(coarse_perm, 'col', axis=1, tiled=True)]
    reduce_sum x6 -> x0, other arithmetic: 15.3 us -> none  [coarsen(): field.reshape(size_x // 2, 2, size_y // 2, 2, size_z // 2, 2)]
    add x28 -> x0, other arithmetic: 11.6 us -> none  [the longest x25 11.6 us: jacobi_sweep(): pressure + OMEGA * (right_side - apply_operator(padder(pressure), pressur...]
    mul x7 -> x0, other arithmetic: 6.25 us -> none  [the longest x4 3.97 us: coefficients(): above = jnp.concatenate([inner, 2.0 * center[:, :, -1:] * scale], axis=2)]
  transfers between devices with their start and end apart: 96 -> 0, of which waited for: 62 -> 0; matrix products, arithmetic and copies ran while one was open for 24% -> 0% of each run, Pallas kernels for 0% -> 0%
where the time goes in v2:
time: 38.2 us; the launch traced here: 38 us
  Pallas kernels  36.3 us (95%)
  local copies, waits for them, and re-layouts  1.67 us (4%)
    pallas_call x1, Pallas kernels, on_device(): pl.pallas_call(functools.partial(cycle_kernel, sizes, (fine, mid)), out_s...  36.3 us
    unnamed x1, local copies, waits for them, and re-layouts  1.67 us

profile of v2, /device:TPU:0, one launch (start us, length us, event | category | flops | bytes accessed | tf_op | source)
XLA Modules:
  0.0 38.0 jit_solution(14428364132304916749)
XLA Ops:
  0.0 36.3 %shard_map.37 = f32[32,16,128]{2,1,0:T(8,128)} custom-call(f32[32,16,128]{2,1,0:T(8,128)} %p_hbm.1, f32[32,16,128]{2,1,0:T(8,128)} %s_hbm.1, f32[32,16,128]{2,1,0:T(8,128)} %k_hbm.1), custom_call_target="tpu_custom_call" | custom-call | tf_op jit(solution)/shard_map/pallas_call | solution.py:665
  36.3 1.7 %copy.5 = f32[32,16,128]{2,1,0:T(8,128)} copy(f32[32,16,128]{2,1,0:T(8,128)} %shard_map.37) | data formatting | bytes 524288

commit v3 on v2

--- a/solution.py
+++ b/solution.py
@@ -471,13 +471,6 @@
 
     loads[0].wait()
     bring([(k_in, kw)])
-    loads[1].wait()
-    loads[2].wait()
-    bring([(p_in, pw), (s_in, sw)])
-    pl.semaphore_wait(barrier, tiles - 1)
-    halo_k = exchange(fine, [(kw, 3)], bufs[0])
-    halo_p = exchange(fine, [(pw, 3), (sw, 2)], bufs[1])
-
     def halves(slot, value, n):
         at = slot * sub
         tmp[at:at + value.shape[0], :] = value
@@ -510,12 +503,17 @@
     lo, hi, lo1, hi1 = PAD, PAD + nx, PAD, PAD + mid.nx
     to_tile([k1[mid.at(x), :] for x in range(lo1, hi1)], tile_k)
     k2[0:8, :] = tile_k[...]
-    gather(tile_k, k2, (gsend.at[0], grecv.at[0]), sizes, ids)
-    halo_k1 = exchange(mid, [(k1, 3)], bufs[2])
-
+    loads[1].wait()
+    loads[2].wait()
+    bring([(p_in, pw), (s_in, sw)])
+    pl.semaphore_wait(barrier, tiles - 1)
+    halo_k = exchange(fine, [(kw, 3)], bufs[0])
+    halo_p = exchange(fine, [(pw, 3), (sw, 2)], bufs[1])
     halo_k.finish()
     fine.faces(kw, *faces0, lo - 2, hi + 2, 6)
     halo_p.finish()
+    halo_k1 = exchange(mid, [(k1, 3)], bufs[2])
+    gather(tile_k, k2, (gsend.at[0], grecv.at[0]), sizes, ids)
 
     def put(win, ref):
         def store(x, value):
@@ -562,8 +560,6 @@
     b2[0:8, :] = tile_b[...]
     gather(tile_b, b2, (gsend.at[1], grecv.at[1]), sizes, ids)
     keep(mid, vb, v1)
-    halo_v1 = exchange(mid, [(v1, 3)], bufs[4])
-    halo_vw = exchange(fine, [(vw, 2)], bufs[5])
 
     gather_wait(k2, tiles, (gsend.at[0], grecv.at[0]), ids)
     coarse2.faces(k2, *faces2)
@@ -579,6 +575,8 @@
             faces3[n, side] = value
 
     gather_wait(b2, tiles, (gsend.at[1], grecv.at[1]), ids)
+    halo_v1 = exchange(mid, [(v1, 3)], bufs[4])
+    halo_vw = exchange(fine, [(vw, 2)], bufs[5])
     coarse2.start(p2a, b2, faces2[4])
     coarse2.sweep(p2a, p2b, b2, faces2)
 
@@ -639,10 +637,14 @@
     lax.fori_loop(0, (mid.nx + 2) // 6, correct0, 0)
     fine.sweep(pa, sw, faces0, lo - 1, hi + 1, 9, put(fine, pb))
 
-    def give(x, value):
-        out[x - PAD] = value[0:ny, :]
-
-    fine.sweep(pb, sw, faces0, lo, hi, 8, give)
+    def last(xs):
+        rest = (1.0 - OMEGA) / OMEGA
+        new = [rest * own + (sw[fine.at(x), :] + total) / faces0[3][fine.at(x), :]
+               for x, (own, total) in zip(xs, fine.beside(xs, pb, *faces0[:3]))]
+        for x, value in zip(xs, new):
+            out[x - PAD] = value[0:ny, :]
+
+    fine.groups(lo, hi, 8, last)
 
 
 def on_device(sizes, pressure_in, source, permeability):
@@ -662,7 +664,7 @@
     for win, halos in ((fine, (3,)), (fine, (3, 2)), (mid, (3,)), (mid, (2,)), (mid, (3,)), (fine, (2,))):
         scratch += [pltpu.VMEM(size, jnp.float32) for size in stage_sizes(win, halos)]
     anywhere = pl.BlockSpec(memory_space=pl.ANY)
-    return pl.pallas_call(
+    scaled = pl.pallas_call(
         functools.partial(cycle_kernel, sizes, (fine, mid)),
         out_shape=jax.ShapeDtypeStruct(pressure_in.shape, jnp.float32),
         in_specs=[anywhere] * 3,
@@ -671,6 +673,7 @@
         compiler_params=pltpu.CompilerParams(
             collective_id=0, has_side_effects=True, vmem_limit_bytes=58 * 1024 * 1024),
     )(pressure_in, source, permeability)
+    return OMEGA * scaled
 
 
 def solution(mesh):

time: 38.2 us -> 38.7 us (1.013)
  other arithmetic: 0 us -> 1.68 us
  local copies, waits for them, and re-layouts: 1.67 us -> 0 us
  Pallas kernels: 36.3 us -> 36.9 us
    mul x0 -> x1, other arithmetic: none -> 1.68 us  [on_device(): return OMEGA * scaled]
    unnamed x1 -> x0, local copies, waits for them, and re-layouts: 1.67 us -> none
    pallas_call x1, Pallas kernels: 36.3 us -> 36.9 us  [on_device(): pl.pallas_call(functools.partial(cycle_kernel, sizes, (fine, mid)), out_s...]
where the time goes in v3:
time: 38.7 us; the launch traced here: 38.6 us
  Pallas kernels  36.9 us (95%)
  other arithmetic  1.68 us (4%)
    pallas_call x1, Pallas kernels, on_device(): pl.pallas_call(functools.partial(cycle_kernel, sizes, (fine, mid)), out_s...  36.9 us
    mul x1, other arithmetic, on_device(): return OMEGA * scaled  1.68 us

profile of v3, /device:TPU:0, one launch (start us, length us, event | category | flops | bytes accessed | tf_op | source)
XLA Modules:
  0.0 38.6 jit_solution(7100254567002126802)
XLA Ops:
  0.0 36.9 %shard_map.37 = f32[32,16,128]{2,1,0:T(8,128)} custom-call(f32[32,16,128]{2,1,0:T(8,128)} %p_hbm.1, f32[32,16,128]{2,1,0:T(8,128)} %s_hbm.1, f32[32,16,128]{2,1,0:T(8,128)} %k_hbm.1), custom_call_target="tpu_custom_call" | custom-call | tf_op jit(solution)/shard_map/pallas_call | solution.py:667
  36.9 1.7 %broadcast_multiply_fusion = f32[32,16,128]{2,1,0:T(8,128)} fusion(f32[32,16,128]{2,1,0:T(8,128)} %shard_map.37), kind=kLoop, calls=%fused_computation | loop fusion | flops 65536 | bytes 524288 | tf_op jit(solution)/shard_map/mul | solution.py:676

commit v4 on v3

--- a/solution.py
+++ b/solution.py
@@ -112,25 +112,31 @@
 
 class Packed:
     def __init__(self, rows, cols):
-        self.rows, self.cols, self.sub = rows, cols, cols * 8
+        self.rows, self.cols, self.sub = rows, cols, cols * 4
         self.scale = 0.25**2
 
     def at(self, r):
-        return pl.ds(pl.multiple_of(r * self.sub, 8), self.sub)
-
-    def west(self, here, before):
+        start = r * self.sub
+        return pl.ds(start if isinstance(r, int) else pl.multiple_of(start, 8), self.sub)
+
+    def landed(self, ref, r):
+        start = pl.multiple_of(r * self.sub * 2, 8)
+        return [ref[pl.ds(start + i, self.sub, stride=2), :] for i in range(2)]
+
+    def load(self, ref, r):
+        return [ref[i, self.at(r), :] for i in range(2)]
+
+    def save(self, ref, r, pair):
+        for i in range(2):
+            ref[i, self.at(r), :] = pair[i]
+
+    def west(self, before, here):
         j = lane_ids(self.sub) % 4
-        odd = row_ids(self.sub) % 2 == 1
-        up, up_before = roll(here, -1, 0), roll(before, -1, 0)
-        other = jnp.where(j > 0, roll(up, 1, 1), roll(up_before, -3, 1))
-        return jnp.where(odd, roll(here, 1, 0), other)
+        return [jnp.where(j > 0, roll(here[1], 1, 1), roll(before[1], -3, 1)), here[0]]
 
     def east(self, here, after):
         j = lane_ids(self.sub) % 4
-        odd = row_ids(self.sub) % 2 == 1
-        down, down_after = roll(here, 1, 0), roll(after, 1, 0)
-        other = jnp.where(j < 3, roll(down, -1, 1), roll(down_after, 3, 1))
-        return jnp.where(odd, other, roll(here, -1, 0))
+        return [here[1], jnp.where(j < 3, roll(here[0], -1, 1), roll(after[0], 3, 1))]
 
     def groups(self, body):
         size = 4 if self.rows % 4 == 0 else 1
@@ -144,56 +150,61 @@
     def around(self, rows):
         return [lax.rem(rows[0] + self.rows - 1, self.rows)] + rows + [lax.rem(rows[-1] + 1, self.rows)]
 
-    def faces(self, perm, cx, cy, cz, diag, weight):
+    def faces(self, landed, cx, cy, cz, diag, weight):
         lane = lane_ids(self.sub)
 
         def first(rows):
-            ks = [perm[self.at(r), :] for r in self.around(rows)]
-            new = [harmonic(self.west(k, before), k, self.scale) for before, k in zip(ks, ks[1:-1])]
-            for r, value in zip(rows, new):
-                cx[self.at(r), :] = value
+            ks = [self.landed(landed, r) for r in self.around(rows)]
+            new = [[harmonic(w, k, self.scale) for w, k in zip(self.west(before, here), here)]
+                   for before, here in zip(ks, ks[1:-1])]
+            for r, pair in zip(rows, new):
+                self.save(cx, r, pair)
 
         self.groups(first)
 
         def second(rows):
-            west = [cx[self.at(r), :] for r in self.around(rows)]
+            west = [self.load(cx, r) for r in self.around(rows)]
             found = []
-            for i, r in enumerate(rows):
-                k = perm[self.at(r), :]
-                south = harmonic(roll(k, 2, 0), k, self.scale)
-                under = jnp.where(lane < 4, 0.0, harmonic(roll(k, 4, 1), k, self.scale))
-                outer = 2.0 * k * self.scale
-                below = jnp.where(lane < 4, outer, under)
-                above = jnp.where(lane >= 124, outer, roll(under, -4, 1))
-                total = west[i + 1] + self.east(west[i + 1], west[i + 2])
-                total = total + south + roll(south, -2, 0) + below + above
-                found.append((south, under, total, OMEGA / total))
-            for r, (south, under, total, inverse) in zip(rows, found):
-                cy[self.at(r), :] = south
-                cz[self.at(r), :] = under
-                diag[self.at(r), :] = total
-                weight[self.at(r), :] = inverse
+            for n, r in enumerate(rows):
+                east = self.east(west[n + 1], west[n + 2])
+                both = []
+                for i, k in enumerate(self.landed(landed, r)):
+                    south = harmonic(roll(k, 1, 0), k, self.scale)
+                    under = jnp.where(lane < 4, 0.0, harmonic(roll(k, 4, 1), k, self.scale))
+                    outer = 2.0 * k * self.scale
+                    below = jnp.where(lane < 4, outer, under)
+                    above = jnp.where(lane >= 124, outer, roll(under, -4, 1))
+                    total = west[n + 1][i] + east[i] + south + roll(south, -1, 0) + below + above
+                    both.append((south, under, total, OMEGA / total))
+                found.append(list(zip(*both)))
+            for r, values in zip(rows, found):
+                for ref, pair in zip((cy, cz, diag, weight), values):
+                    self.save(ref, r, pair)
 
         self.groups(second)
 
     def beside(self, rows, v, cx, cy, cz):
-        vs = [v[self.at(r), :] for r in self.around(rows)]
-        west = [cx[self.at(r), :] for r in self.around(rows)]
-        flow = [c * value for c, value in zip(west[1:], vs[1:])]
+        vs = [self.load(v, r) for r in self.around(rows)]
+        west = [self.load(cx, r) for r in self.around(rows)]
+        flow = [[c * value for c, value in zip(cs, both)] for cs, both in zip(west, vs)]
         out = []
-        for i, r in enumerate(rows):
-            own, south, under = vs[i + 1], cy[self.at(r), :], cz[self.at(r), :]
-            total = west[i + 1] * self.west(own, vs[i]) + self.east(flow[i], flow[i + 1])
-            total = total + (south * roll(own, 2, 0) + roll(south * own, -2, 0))
-            total = total + (under * roll(own, 4, 1) + roll(under * own, -4, 1))
-            out.append((own, total))
+        for n, r in enumerate(rows):
+            lower, upper = self.west(vs[n], vs[n + 1]), self.east(flow[n + 1], flow[n + 2])
+            souths, unders, pair = self.load(cy, r), self.load(cz, r), []
+            for i in range(2):
+                own, south, under = vs[n + 1][i], souths[i], unders[i]
+                total = west[n + 1][i] * lower[i] + upper[i]
+                total = total + (south * roll(own, 1, 0) + roll(south * own, -1, 0))
+                total = total + (under * roll(own, 4, 1) + roll(under * own, -4, 1))
+                pair.append((own, total))
+            out.append(pair)
         return out
 
     def start(self, v, rhs, weight):
         def body(rows):
-            new = [weight[self.at(r), :] * rhs[self.at(r), :] for r in rows]
-            for r, value in zip(rows, new):
-                v[self.at(r), :] = value
+            new = [[w * b for w, b in zip(self.load(weight, r), self.landed(rhs, r))] for r in rows]
+            for r, pair in zip(rows, new):
+                self.save(v, r, pair)
 
         self.groups(body)
 
@@ -201,100 +212,73 @@
         cx, cy, cz, _, weight = faces
 
         def body(rows):
-            values = [(1.0 - OMEGA) * own + weight[self.at(r), :] * (rhs[self.at(r), :] + total)
-                      for r, (own, total) in zip(rows, self.beside(rows, v, cx, cy, cz))]
-            for r, value in zip(rows, values):
-                new[self.at(r), :] = value
+            values = []
+            for r, found in zip(rows, self.beside(rows, v, cx, cy, cz)):
+                parts = zip(found, self.load(weight, r), self.landed(rhs, r))
+                values.append([(1.0 - OMEGA) * own + w * (b + total) for (own, total), w, b in parts])
+            for r, pair in zip(rows, values):
+                self.save(new, r, pair)
 
         self.groups(body)
 
-    def block_mean(self, value):
-        row = row_ids(self.sub)
-        value = value + jnp.where(row % 2 == 0, roll(value, -1, 0), roll(value, 1, 0))
-        value = value + jnp.where(row // 2 % 2 == 0, roll(value, -2, 0), roll(value, 2, 0))
+    def block_mean(self, pair):
+        value = pair[0] + pair[1]
+        low = row_ids(self.sub) % 2 == 0
+        value = value + jnp.where(low, roll(value, -1, 0), roll(value, 1, 0))
         return pair_sum(value, 4) * 0.125
 
 
 class Coarsest:
     def __init__(self, rows, cols):
-        self.g, self.q, self.sub = rows // 2, cols // 4, cols * 8
-        self.cells = [(g, q) for g in range(self.g) for q in range(self.q)]
+        self.count, self.sub = rows // 2, cols * 2
+        self.cells = range(self.count)
         self.scale = 0.25**3
 
-    def at(self, r, c):
-        return pl.ds(r * self.sub + c * 8, 8)
-
     def pack(self, ref):
-        sublane, lane = row_ids(8) % 4, lane_ids(8) // 4 % 2
-        out = {}
-        for g, q in self.cells:
-            halves = []
-            for r in (2 * g, 2 * g + 1):
-                half = ref[self.at(r, 4 * q), :]
-                for c in (1, 2, 3):
-                    half = jnp.where(sublane == c, ref[self.at(r, 4 * q + c), :], half)
-                halves.append(half)
-            out[g, q] = jnp.where(lane == 0, halves[0], halves[1])
+        low = lane_ids(self.sub) // 4 % 2 == 0
+        parts = [ref[pl.ds(r * self.sub * 2, self.sub, stride=2), :] for r in range(2 * self.count)]
+        return [jnp.where(low, parts[2 * g], parts[2 * g + 1]) for g in self.cells]
+
+    def repeated(self, v, r):
+        mine = lane_ids(self.sub) // 4 % 2 == r % 2
+        return jnp.where(mine, v[r // 2], roll(v[r // 2], 4 if r % 2 == 0 else -4, 1))
+
+    def lower_x(self, v, g):
+        return jnp.where(lane_ids(self.sub) % 8 > 0, roll(v[g], 1, 1), roll(v[g - 1], -7, 1))
+
+    def upper_x(self, v, g):
+        after = v[(g + 1) % self.count]
+        return jnp.where(lane_ids(self.sub) % 8 < 7, roll(v[g], -1, 1), roll(after, 7, 1))
+
+    def faces(self, k):
+        lane = lane_ids(self.sub)
+        cx = [harmonic(self.lower_x(k, g), k[g], self.scale) for g in self.cells]
+        out = []
+        for g in self.cells:
+            south = harmonic(roll(k[g], 1, 0), k[g], self.scale)
+            under = jnp.where(lane < 8, 0.0, harmonic(roll(k[g], 8, 1), k[g], self.scale))
+            over = jnp.where(lane >= 120, 0.0, roll(under, -8, 1))
+            outer = 2.0 * k[g] * self.scale
+            below, above = jnp.where(lane < 8, outer, under), jnp.where(lane >= 120, outer, over)
+            east, north = self.upper_x(cx, g), roll(south, -1, 0)
+            total = cx[g] + east + south + north + below + above
+            weight = OMEGA / total
+            out.append([weight * c for c in (cx[g], east, south, north, under, over)] + [weight])
         return out
 
-    def repeated(self, v, r, c):
-        value = v[r // 2, c // 4]
-        high = lane_ids(8) // 4 % 2
-        value = jnp.where(high == r % 2, value, roll(value, 4 if r % 2 == 0 else -4, 1))
-        row = row_ids(8)
-        value = jnp.where(row % 4 == c % 4, value, 0.0)
-        value = value + jnp.where(row % 2 == 0, roll(value, -1, 0), roll(value, 1, 0))
-        return value + jnp.where(row // 2 % 2 == 0, roll(value, -2, 0), roll(value, 2, 0))
-
-    def lower_x(self, v, g, q):
-        here = lane_ids(8) % 8 > 0
-        return jnp.where(here, roll(v[g, q], 1, 1), roll(v[(g - 1) % self.g, q], -7, 1))
-
-    def upper_x(self, v, g, q):
-        here = lane_ids(8) % 8 < 7
-        return jnp.where(here, roll(v[g, q], -1, 1), roll(v[(g + 1) % self.g, q], 7, 1))
-
-    def lower_y(self, v, g, q):
-        row = row_ids(8)
-        other = jnp.where(row == 0, roll(v[g, (q - 1) % self.q], 1, 0), roll(v[g, q], -3, 0))
-        return jnp.where(row >= 4, roll(v[g, q], 4, 0), other)
-
-    def upper_y(self, v, g, q):
-        row = row_ids(8)
-        other = jnp.where(row == 7, roll(v[g, (q + 1) % self.q], -1, 0), roll(v[g, q], 3, 0))
-        return jnp.where(row < 4, roll(v[g, q], 4, 0), other)
-
-    def faces(self, k):
-        lane = lane_ids(8)
-        cx = {i: harmonic(self.lower_x(k, *i), k[i], self.scale) for i in self.cells}
-        cy = {i: harmonic(self.lower_y(k, *i), k[i], self.scale) for i in self.cells}
-        out = {}
-        for i in self.cells:
-            under = jnp.where(lane < 8, 0.0, harmonic(roll(k[i], 8, 1), k[i], self.scale))
-            over = jnp.where(lane >= 120, 0.0, roll(under, -8, 1))
-            outer = 2.0 * k[i] * self.scale
-            below, above = jnp.where(lane < 8, outer, under), jnp.where(lane >= 120, outer, over)
-            east, north = self.upper_x(cx, *i), self.upper_y(cy, *i)
-            total = cx[i] + east + cy[i] + north + below + above
-            weight = OMEGA / total
-            out[i] = [weight * c for c in (cx[i], east, cy[i], north, under, over)] + [weight]
-        return out
-
     def solve(self, faces, rhs):
-        start = {i: faces(i, 6) * rhs[i] for i in self.cells}
-
-        def sweep(_, carry):
-            v = dict(zip(self.cells, carry))
+        start = [faces(g, 6) * rhs[g] for g in self.cells]
+
+        def sweep(_, v):
             new = []
-            for i in self.cells:
-                side_x = faces(i, 0) * self.lower_x(v, *i) + faces(i, 1) * self.upper_x(v, *i)
-                side_y = faces(i, 2) * self.lower_y(v, *i) + faces(i, 3) * self.upper_y(v, *i)
-                side_z = faces(i, 4) * roll(v[i], 8, 1) + faces(i, 5) * roll(v[i], -8, 1)
-                new.append(((1.0 - OMEGA) * v[i] + start[i] + side_z) + (side_x + side_y))
+            for g in self.cells:
+                side_x = faces(g, 0) * self.lower_x(v, g) + faces(g, 1) * self.upper_x(v, g)
+                side_y = faces(g, 2) * roll(v[g], 1, 0) + faces(g, 3) * roll(v[g], -1, 0)
+                side_z = faces(g, 4) * roll(v[g], 8, 1) + faces(g, 5) * roll(v[g], -8, 1)
+                new.append(((1.0 - OMEGA) * v[g] + start[g] + side_z) + (side_x + side_y))
             return tuple(new)
 
-        done = lax.fori_loop(1, CSWEEPS, sweep, tuple(start[i] for i in self.cells))
-        return dict(zip(self.cells, done))
+        return lax.fori_loop(1, CSWEEPS, sweep, tuple(start))
 
 
 class Exchange:
@@ -422,12 +406,12 @@
         got, scratch[:count] = scratch[:count], []
         return got
 
-    p_in, s_in, k_in, in_sems = take(4)
+    p_in, s_in, k_in, in_sems, out_sems = take(5)
     pw, pa, pb, sw, kw, vw = take(6)
     faces0 = take(5)
     b1, k1, va, vb, v1 = take(5)
     faces1 = take(5)
-    k2, b2, p2a, p2b, b3 = take(5)
+    k2, b2, b3, p2a, p2b = take(5)
     faces2 = take(5)
     faces3 = take(1)[0]
     tmp, tile_b, tile_k = take(3)
@@ -471,6 +455,13 @@
 
     loads[0].wait()
     bring([(k_in, kw)])
+    loads[1].wait()
+    loads[2].wait()
+    bring([(p_in, pw), (s_in, sw)])
+    pl.semaphore_wait(barrier, tiles - 1)
+    halo_k = exchange(fine, [(kw, 3)], bufs[0])
+    halo_p = exchange(fine, [(pw, 3), (sw, 2)], bufs[1])
+
     def halves(slot, value, n):
         at = slot * sub
         tmp[at:at + value.shape[0], :] = value
@@ -503,12 +494,6 @@
     lo, hi, lo1, hi1 = PAD, PAD + nx, PAD, PAD + mid.nx
     to_tile([k1[mid.at(x), :] for x in range(lo1, hi1)], tile_k)
     k2[0:8, :] = tile_k[...]
-    loads[1].wait()
-    loads[2].wait()
-    bring([(p_in, pw), (s_in, sw)])
-    pl.semaphore_wait(barrier, tiles - 1)
-    halo_k = exchange(fine, [(kw, 3)], bufs[0])
-    halo_p = exchange(fine, [(pw, 3), (sw, 2)], bufs[1])
     halo_k.finish()
     fine.faces(kw, *faces0, lo - 2, hi + 2, 6)
     halo_p.finish()
@@ -565,14 +550,14 @@
     coarse2.faces(k2, *faces2)
 
     def k_coarsest(rs):
-        new = [coarse2.block_mean(k2[coarse2.at(r), :]) for r in rs]
+        new = [coarse2.block_mean(coarse2.landed(k2, r)) for r in rs]
         for r, value in zip(rs, new):
             b3[coarse2.at(r), :] = value
 
     coarse2.groups(k_coarsest)
-    for n, group in enumerate(coarse3.faces(coarse3.pack(b3)).values()):
+    for g, group in enumerate(coarse3.faces(coarse3.pack(b3))):
         for side, value in enumerate(group):
-            faces3[n, side] = value
+            faces3[g, side] = value
 
     gather_wait(b2, tiles, (gsend.at[1], grecv.at[1]), ids)
     halo_v1 = exchange(mid, [(v1, 3)], bufs[4])
@@ -581,32 +566,37 @@
     coarse2.sweep(p2a, p2b, b2, faces2)
 
     def restrict2(rs):
-        new = [coarse2.block_mean(b2[coarse2.at(r), :] - faces2[3][coarse2.at(r), :] * own + total)
-               for r, (own, total) in zip(rs, coarse2.beside(rs, p2b, *faces2[:3]))]
+        new = []
+        for r, found in zip(rs, coarse2.beside(rs, p2b, *faces2[:3])):
+            parts = zip(found, coarse2.load(faces2[3], r), coarse2.landed(b2, r))
+            new.append(coarse2.block_mean([b - d * own + total for (own, total), d, b in parts]))
         for r, value in zip(rs, new):
             b3[coarse2.at(r), :] = value
 
     coarse2.groups(restrict2)
-    e3 = coarse3.solve(lambda i, side: faces3[coarse3.cells.index(i), side], coarse3.pack(b3))
+    e3 = coarse3.solve(lambda g, side: faces3[g, side], coarse3.pack(b3))
     for r in range(rows):
-        for c in range(cols):
-            at = coarse3.at(r, c)
-            p2a[at, :] = p2b[at, :] + coarse3.repeated(e3, r, c)
+        value = coarse3.repeated(e3, r)
+        for half in range(2):
+            b3[pl.ds(r * coarse2.sub + half, coarse3.sub, stride=2), :] = value
+
+    def correct2(rs):
+        new = [[value + b3[coarse2.at(r), :] for value in coarse2.load(p2b, r)] for r in rs]
+        for r, pair in zip(rs, new):
+            coarse2.save(p2a, r, pair)
+
+    coarse2.groups(correct2)
     coarse2.sweep(p2a, p2b, b2, faces2)
     coarse2.sweep(p2b, p2a, b2, faces2)
 
     halo_v1.finish()
     span = coarse2.sub
     lane = lane_ids(span)
-    places = ((-1, 3), (0, 0), (0, 1), (0, 2), (0, 3), (1, 0))
-    for n, (dr, j) in enumerate(places):
-        part = p2a[(dr % rows) * span:(dr % rows + 1) * span, :]
-        part = pair_sum(pair_sum(jnp.where(lane % 4 == j, part, 0.0), 1), 2)
-        turned = roll(part, 16 - span, 0)
-        tmp[16 * n:16 * n + 16, :] = jnp.where(row_ids(16) < 12, part[0:16, :], turned[0:16, :])
-    for n, (dr, j) in enumerate(places):
-        for i in range(2):
-            e = tmp[pl.ds(16 * n + i, 8, stride=2), :]
+    for dr, j in ((-1, 3), (0, 0), (0, 1), (0, 2), (0, 3), (1, 0)):
+        for i, part in enumerate(coarse2.load(p2a, dr % rows)):
+            part = pair_sum(pair_sum(jnp.where(lane % 4 == j, part, 0.0), 1), 2)
+            turned = roll(part, 8 - span, 0)
+            e = jnp.where(row_ids(8) < 6, part[0:8, :], turned[0:8, :])
             x = 2 * (8 * dr + 2 * j + i) + PAD
             for row in (x, x + 1):
                 for half in range(2):
@@ -642,9 +632,17 @@
         new = [rest * own + (sw[fine.at(x), :] + total) / faces0[3][fine.at(x), :]
                for x, (own, total) in zip(xs, fine.beside(xs, pb, *faces0[:3]))]
         for x, value in zip(xs, new):
-            out[x - PAD] = value[0:ny, :]
-
-    fine.groups(lo, hi, 8, last)
+            p_in[x - PAD] = value[0:ny, :]
+
+    part = nx // 4
+    writes = []
+    for n in range(4):
+        fine.groups(lo + n * part, lo + (n + 1) * part, part, last)
+        span = pl.ds(n * part, part)
+        writes.append(pltpu.make_async_copy(p_in.at[span], out.at[span], out_sems.at[n]))
+        writes[-1].start()
+    for write in writes:
+        write.wait()
 
 
 def on_device(sizes, pressure_in, source, permeability):
@@ -656,9 +654,10 @@
         return pltpu.VMEM(((win.nx + 2 * PAD) * win.sub, 128), jnp.float32)
 
     packed = pltpu.VMEM((rows * cols * 8, 128), jnp.float32)
-    scratch = [pltpu.VMEM(pressure_in.shape, jnp.float32)] * 3 + [pltpu.SemaphoreType.DMA((3,))]
-    scratch += [window(fine)] * 11 + [window(mid)] * 10 + [packed] * 10
-    scratch += [pltpu.VMEM((rows * cols // 8, 7, 8, 128), jnp.float32)]
+    halved = pltpu.VMEM((2, rows * cols * 4, 128), jnp.float32)
+    scratch = [pltpu.VMEM(pressure_in.shape, jnp.float32)] * 3 + [pltpu.SemaphoreType.DMA((3,)), pltpu.SemaphoreType.DMA((4,))]
+    scratch += [window(fine)] * 11 + [window(mid)] * 10 + [packed] * 3 + [halved] * 7
+    scratch += [pltpu.VMEM((rows // 2, 7, cols * 2, 128), jnp.float32)]
     scratch += [pltpu.VMEM((8 * fine.sub, 128), jnp.float32)] + [pltpu.VMEM((8, 128), jnp.float32)] * 2
     scratch += [pltpu.SemaphoreType.DMA((64,))] * 2 + [pltpu.SemaphoreType.DMA((2,))] * 2
     for win, halos in ((fine, (3,)), (fine, (3, 2)), (mid, (3,)), (mid, (2,)), (mid, (3,)), (fine, (2,))):
@@ -667,11 +666,11 @@
     scaled = pl.pallas_call(
         functools.partial(cycle_kernel, sizes, (fine, mid)),
         out_shape=jax.ShapeDtypeStruct(pressure_in.shape, jnp.float32),
-        in_specs=[anywhere] * 3,
-        out_specs=pl.BlockSpec(memory_space=pltpu.VMEM),
+        in_specs=[pl.BlockSpec(memory_space=pltpu.HBM)] * 3,
+        out_specs=anywhere,
         scratch_shapes=scratch,
         compiler_params=pltpu.CompilerParams(
-            collective_id=0, has_side_effects=True, vmem_limit_bytes=58 * 1024 * 1024),
+            collective_id=0, has_side_effects=True, vmem_limit_bytes=(24 if rows * cols <= 64 else 56) * 1024 * 1024),
     )(pressure_in, source, permeability)
     return OMEGA * scaled
 

time: 38.7 us -> 40.5 us (1.047)
  local copies, waits for them, and re-layouts: 0 us -> 2.85 us
  other arithmetic: 1.68 us -> 0.73 us
    unnamed x0 -> x6, local copies, waits for them, and re-layouts: none -> 2.85 us
    mul x1, other arithmetic: 1.68 us -> 0.73 us  [on_device(): return OMEGA * scaled]
where the time goes in v4:
time: 40.5 us; the launch traced here: 40.3 us
  Pallas kernels  36.7 us (91%)
  local copies, waits for them, and re-layouts  2.85 us (7%)
  other arithmetic  0.73 us (2%)
    pallas_call x1, Pallas kernels, on_device(): pl.pallas_call(functools.partial(cycle_kernel, sizes, (fine, mid)), out_s...  36.7 us
    unnamed x6, local copies, waits for them, and re-layouts  2.85 us

profile of v4, /device:TPU:0, one launch (start us, length us, event | category | flops | bytes accessed | tf_op | source)
XLA Modules:
  0.0 40.3 jit_solution(9570572924420542802)
XLA Ops:
  0.0 0.0 copy-start
  0.0 0.9 %copy-done = f32[32,16,128]{2,1,0:T(8,128)S(1)} copy-done((f32[32,16,128]{2,1,0:T(8,128)S(1)}, f32[32,16,128]{2,1,0:T(8,128)}, u32[]{:S(2)}) %copy-start) | copy-done | bytes 262168
  1.0 0.0 copy-start.1
  1.0 0.9 %copy-done.1 = f32[32,16,128]{2,1,0:T(8,128)S(1)} copy-done((f32[32,16,128]{2,1,0:T(8,128)S(1)}, f32[32,16,128]{2,1,0:T(8,128)}, u32[]{:S(2)}) %copy-start.1) | copy-done | bytes 262168
  1.9 0.0 copy-start.2
  1.9 0.9 %copy-done.2 = f32[32,16,128]{2,1,0:T(8,128)S(1)} copy-done((f32[32,16,128]{2,1,0:T(8,128)S(1)}, f32[32,16,128]{2,1,0:T(8,128)}, u32[]{:S(2)}) %copy-start.2) | copy-done | bytes 262168
  2.9 36.7 %shard_map.37 = f32[32,16,128]{2,1,0:T(8,128)S(1)} custom-call(f32[32,16,128]{2,1,0:T(8,128)S(1)} %copy-done, f32[32,16,128]{2,1,0:T(8,128)S(1)} %copy-done.1, f32[32,16,128]{2,1,0:T(8,128)S(1)} %copy-done.2), custom_call_target="tpu_custom_call" | custom-call | tf_op jit(solution)/shard_map/pallas_call | solution.py:666
  39.6 0.7 %broadcast_multiply_fusion = f32[32,16,128]{2,1,0:T(8,128)} fusion(f32[32,16,128]{2,1,0:T(8,128)S(1)} %shard_map.37), kind=kLoop, calls=%fused_computation | loop fusion | flops 65536 | bytes 524288 | tf_op jit(solution)/shard_map/mul | solution.py:675
Async XLA Ops:
  0.0 0.9 %copy-start = (f32[32,16,128]{2,1,0:T(8,128)S(1)}, f32[32,16,128]{2,1,0:T(8,128)}, u32[]{:S(2)}) copy-start(f32[32,16,128]{2,1,0:T(8,128)} %p_hbm.1) | copy-start | bytes 786436
  1.0 0.9 %copy-start.1 = (f32[32,16,128]{2,1,0:T(8,128)S(1)}, f32[32,16,128]{2,1,0:T(8,128)}, u32[]{:S(2)}) copy-start(f32[32,16,128]{2,1,0:T(8,128)} %s_hbm.1) | copy-start | bytes 786436
  1.9 0.9 %copy-start.2 = (f32[32,16,128]{2,1,0:T(8,128)S(1)}, f32[32,16,128]{2,1,0:T(8,128)}, u32[]{:S(2)}) copy-start(f32[32,16,128]{2,1,0:T(8,128)} %k_hbm.1) | copy-start | bytes 786436

commit v5 on v4

--- a/solution.py
+++ b/solution.py
@@ -139,7 +139,7 @@
         return [here[1], jnp.where(j < 3, roll(here[0], -1, 1), roll(after[0], 3, 1))]
 
     def groups(self, body):
-        size = 4 if self.rows % 4 == 0 else 1
+        size = 8 if self.rows % 8 == 0 else 1
 
         def step(g, carry):
             body([g * size + i for i in range(size)])
@@ -495,7 +495,7 @@
     to_tile([k1[mid.at(x), :] for x in range(lo1, hi1)], tile_k)
     k2[0:8, :] = tile_k[...]
     halo_k.finish()
-    fine.faces(kw, *faces0, lo - 2, hi + 2, 6)
+    fine.faces(kw, *faces0, lo - 2, hi + 2, 9)
     halo_p.finish()
     halo_k1 = exchange(mid, [(k1, 3)], bufs[2])
     gather(tile_k, k2, (gsend.at[0], grecv.at[0]), sizes, ids)
@@ -508,15 +508,15 @@
     def put_both(x, value):
         pb[fine.at(x), :] = value
 
-    fine.sweep(pw, sw, faces0, lo - 2, hi + 2, 9, put(fine, pa))
-    fine.sweep(pa, sw, faces0, lo - 1, hi + 1, 9, put_both)
+    fine.sweep(pw, sw, faces0, lo - 2, hi + 2, 18, put(fine, pa))
+    fine.sweep(pa, sw, faces0, lo - 1, hi + 1, 17, put_both)
 
     def restrict0(i, carry):
-        left = fine.residual([8 * i + PAD + n for n in range(8)], pb, sw, faces0)
-        to_mid(i, b1, [pair_sum(left[2 * n] + left[2 * n + 1], 1) for n in range(4)])
+        left = fine.residual([16 * i + PAD + n for n in range(16)], pb, sw, faces0)
+        to_mid(i, b1, [pair_sum(left[2 * n] + left[2 * n + 1], 1) for n in range(8)])
         return carry
 
-    lax.fori_loop(0, nx // 8, restrict0, 0)
+    lax.fori_loop(0, nx // 16, restrict0, 0)
     halo_b1 = exchange(mid, [(b1, 2)], bufs[3])
 
     def keep(win, src, dst):
@@ -625,7 +625,7 @@
         return carry
 
     lax.fori_loop(0, (mid.nx + 2) // 6, correct0, 0)
-    fine.sweep(pa, sw, faces0, lo - 1, hi + 1, 9, put(fine, pb))
+    fine.sweep(pa, sw, faces0, lo - 1, hi + 1, 17, put(fine, pb))
 
     def last(xs):
         rest = (1.0 - OMEGA) / OMEGA
@@ -634,9 +634,9 @@
         for x, value in zip(xs, new):
             p_in[x - PAD] = value[0:ny, :]
 
-    part = nx // 4
+    part = nx // 2
     writes = []
-    for n in range(4):
+    for n in range(2):
         fine.groups(lo + n * part, lo + (n + 1) * part, part, last)
         span = pl.ds(n * part, part)
         writes.append(pltpu.make_async_copy(p_in.at[span], out.at[span], out_sems.at[n]))
@@ -655,7 +655,7 @@
 
     packed = pltpu.VMEM((rows * cols * 8, 128), jnp.float32)
     halved = pltpu.VMEM((2, rows * cols * 4, 128), jnp.float32)
-    scratch = [pltpu.VMEM(pressure_in.shape, jnp.float32)] * 3 + [pltpu.SemaphoreType.DMA((3,)), pltpu.SemaphoreType.DMA((4,))]
+    scratch = [pltpu.VMEM(pressure_in.shape, jnp.float32)] * 3 + [pltpu.SemaphoreType.DMA((3,)), pltpu.SemaphoreType.DMA((2,))]
     scratch += [window(fine)] * 11 + [window(mid)] * 10 + [packed] * 3 + [halved] * 7
     scratch += [pltpu.VMEM((rows // 2, 7, cols * 2, 128), jnp.float32)]
     scratch += [pltpu.VMEM((8 * fine.sub, 128), jnp.float32)] + [pltpu.VMEM((8, 128), jnp.float32)] * 2
@@ -670,7 +670,7 @@
         out_specs=anywhere,
         scratch_shapes=scratch,
         compiler_params=pltpu.CompilerParams(
-            collective_id=0, has_side_effects=True, vmem_limit_bytes=(24 if rows * cols <= 64 else 56) * 1024 * 1024),
+            collective_id=0, has_side_effects=True, vmem_limit_bytes=56 * 1024 * 1024),
     )(pressure_in, source, permeability)
     return OMEGA * scaled
 

time: 40.5 us -> 38.3 us (0.946)
  local copies, waits for them, and re-layouts: 2.85 us -> 0 us
  other arithmetic: 0.73 us -> 1.68 us
    unnamed x6 -> x0, local copies, waits for them, and re-layouts: 2.85 us -> none
    mul x1, other arithmetic: 0.73 us -> 1.68 us  [on_device(): return OMEGA * scaled]
where the time goes in v5:
time: 38.3 us; the launch traced here: 38.2 us
  Pallas kernels  36.5 us (95%)
  other arithmetic  1.68 us (4%)
    pallas_call x1, Pallas kernels, on_device(): pl.pallas_call(functools.partial(cycle_kernel, sizes, (fine, mid)), out_s...  36.5 us
    mul x1, other arithmetic, on_device(): return OMEGA * scaled  1.68 us

profile of v5, /device:TPU:0, one launch (start us, length us, event | category | flops | bytes accessed | tf_op | source)
XLA Modules:
  0.0 38.2 jit_solution(12070594248359331654)
XLA Ops:
  0.0 36.5 %shard_map.37 = f32[32,16,128]{2,1,0:T(8,128)} custom-call(f32[32,16,128]{2,1,0:T(8,128)} %p_hbm.1, f32[32,16,128]{2,1,0:T(8,128)} %s_hbm.1, f32[32,16,128]{2,1,0:T(8,128)} %k_hbm.1), custom_call_target="tpu_custom_call" | custom-call | tf_op jit(solution)/shard_map/pallas_call | solution.py:666
  36.5 1.7 %broadcast_multiply_fusion = f32[32,16,128]{2,1,0:T(8,128)} fusion(f32[32,16,128]{2,1,0:T(8,128)} %shard_map.37), kind=kLoop, calls=%fused_computation | loop fusion | flops 65536 | bytes 524288 | tf_op jit(solution)/shard_map/mul | solution.py:675

commit v6 on v5

--- a/solution.py
+++ b/solution.py
@@ -360,45 +360,42 @@
     return jnp.where(value >= size, value - size, value)
 
 
-def others(sizes, ids, body):
+def along_cols(sizes, ids, body):
+    (me_r, me_c), cols = ids[0], sizes[1]
+    for c in range(1, cols):
+        body(c, (me_r, wrapped(me_c + cols - c, cols)))
+
+
+def along_rows(sizes, ids, body):
+    (me_r, me_c), rows = ids[0], sizes[0]
+    for r in range(1, rows):
+        body(r, (wrapped(me_r + rows - r, rows), me_c))
+
+
+def gather(src, land, sems, sizes, ids, stage):
+    size = 8 if stage == 0 else 8 * sizes[1]
+
+    def one(slot, to):
+        pltpu.make_async_remote_copy(
+            src_ref=src, dst_ref=land.at[pl.ds(slot * size, size), :], send_sem=sems[0].at[stage],
+            recv_sem=sems[1].at[stage], device_id=to, device_id_type=MESH).start()
+
+    (along_cols if stage == 0 else along_rows)(sizes, ids, one)
+
+
+def gather_wait(land, sems, sizes, ids, stage):
+    (me_r, me_c), (left, _), _ = ids
     rows, cols = sizes
-    me_r, me_c = ids[0]
-    to_cols = [me_c] + [wrapped(me_c + cols - c, cols) for c in range(1, cols)]
-
-    def row(r, carry):
-        to_row = wrapped(me_r + rows - r, rows)
-        for c in range(cols):
-            body(r * cols + c, (to_row, to_cols[c]))
-        return carry
-
-    for c in range(1, cols):
-        body(c, (me_r, to_cols[c]))
-    lax.fori_loop(1, rows, row, 0, unroll=rows <= 8)
-
-
-def gather(src, land, sems, sizes, ids):
-    def one(slot, to):
-        at = slot * 8 if isinstance(slot, int) else pl.multiple_of(slot * 8, 8)
-        pltpu.make_async_remote_copy(
-            src_ref=src, dst_ref=land.at[pl.ds(at, 8), :], send_sem=sems[0], recv_sem=sems[1],
-            device_id=to, device_id_type=MESH).start()
-
-    others(sizes, ids, one)
-
-
-def gather_wait(land, tiles, sems, ids):
-    (me_r, me_c), (left, _), _ = ids
-    span = land.at[pl.ds(8, (tiles - 1) * 8), :]
+    span = pl.ds(8, (cols - 1) * 8) if stage == 0 else pl.ds(cols * 8, (rows - 1) * cols * 8)
     done = pltpu.make_async_remote_copy(
-        src_ref=span, dst_ref=span, send_sem=sems[0], recv_sem=sems[1],
-        device_id=(left, me_c), device_id_type=MESH)
+        src_ref=land.at[span, :], dst_ref=land.at[span, :], send_sem=sems[0].at[stage],
+        recv_sem=sems[1].at[stage], device_id=(left, me_c), device_id_type=MESH)
     done.wait_send()
     done.wait_recv()
 
 
 def cycle_kernel(sizes, wins, p_hbm, s_hbm, k_hbm, out, *scratch):
     rows, cols = sizes
-    tiles = rows * cols
     fine, mid = wins
     scratch = list(scratch)
 
@@ -429,8 +426,14 @@
            (wrapped(me_c + cols - 1, cols), wrapped(me_c + 1, cols)))
 
     barrier = pltpu.get_barrier_semaphore()
-    others(sizes, ids, lambda _, to: pl.semaphore_signal(
-        barrier, inc=1, device_id=to, device_id_type=MESH))
+    def greet(_, to):
+        pl.semaphore_signal(barrier, inc=1, device_id=to, device_id_type=MESH)
+
+    for near_r in ids[1]:
+        for near_c in ids[2]:
+            greet(0, (near_r, near_c))
+    along_cols(sizes, ids, greet)
+    along_rows(sizes, ids, greet)
 
     nx, ny, sub = fine.nx, fine.ny, fine.sub
 
@@ -458,7 +461,7 @@
     loads[1].wait()
     loads[2].wait()
     bring([(p_in, pw), (s_in, sw)])
-    pl.semaphore_wait(barrier, tiles - 1)
+    pl.semaphore_wait(barrier, rows + cols + 2)
     halo_k = exchange(fine, [(kw, 3)], bufs[0])
     halo_p = exchange(fine, [(pw, 3), (sw, 2)], bufs[1])
 
@@ -498,7 +501,8 @@
     fine.faces(kw, *faces0, lo - 2, hi + 2, 9)
     halo_p.finish()
     halo_k1 = exchange(mid, [(k1, 3)], bufs[2])
-    gather(tile_k, k2, (gsend.at[0], grecv.at[0]), sizes, ids)
+    sems_k, sems_b = (gsend.at[0], grecv.at[0]), (gsend.at[1], grecv.at[1])
+    gather(tile_k, k2, sems_k, sizes, ids, 0)
 
     def put(win, ref):
         def store(x, value):
@@ -529,6 +533,8 @@
         lax.fori_loop(0, win.nx // 4, body, 0)
 
     keep(fine, pb, vw)
+    gather_wait(k2, sems_k, sizes, ids, 0)
+    gather(k2.at[pl.ds(0, cols * 8), :], k2, sems_k, sizes, ids, 1)
     halo_k1.finish()
     mid.faces(k1, *faces1, lo1 - 2, hi1 + 2, 10)
     coarse2, coarse3 = Packed(rows, cols), Coarsest(rows, cols)
@@ -543,10 +549,12 @@
     mid.sweep(va, b1, faces1, lo1 - 1, hi1 + 1, 11, put(mid, vb))
     to_tile(mid.residual(list(range(lo1, hi1)), vb, b1, faces1), tile_b)
     b2[0:8, :] = tile_b[...]
-    gather(tile_b, b2, (gsend.at[1], grecv.at[1]), sizes, ids)
+    gather(tile_b, b2, sems_b, sizes, ids, 0)
     keep(mid, vb, v1)
 
-    gather_wait(k2, tiles, (gsend.at[0], grecv.at[0]), ids)
+    gather_wait(b2, sems_b, sizes, ids, 0)
+    gather(b2.at[pl.ds(0, cols * 8), :], b2, sems_b, sizes, ids, 1)
+    gather_wait(k2, sems_k, sizes, ids, 1)
     coarse2.faces(k2, *faces2)
 
     def k_coarsest(rs):
@@ -559,7 +567,7 @@
         for side, value in enumerate(group):
             faces3[g, side] = value
 
-    gather_wait(b2, tiles, (gsend.at[1], grecv.at[1]), ids)
+    gather_wait(b2, sems_b, sizes, ids, 1)
     halo_v1 = exchange(mid, [(v1, 3)], bufs[4])
     halo_vw = exchange(fine, [(vw, 2)], bufs[5])
     coarse2.start(p2a, b2, faces2[4])
@@ -659,7 +667,7 @@
     scratch += [window(fine)] * 11 + [window(mid)] * 10 + [packed] * 3 + [halved] * 7
     scratch += [pltpu.VMEM((rows // 2, 7, cols * 2, 128), jnp.float32)]
     scratch += [pltpu.VMEM((8 * fine.sub, 128), jnp.float32)] + [pltpu.VMEM((8, 128), jnp.float32)] * 2
-    scratch += [pltpu.SemaphoreType.DMA((64,))] * 2 + [pltpu.SemaphoreType.DMA((2,))] * 2
+    scratch += [pltpu.SemaphoreType.DMA((64,))] * 2 + [pltpu.SemaphoreType.DMA((2, 2))] * 2
     for win, halos in ((fine, (3,)), (fine, (3, 2)), (mid, (3,)), (mid, (2,)), (mid, (3,)), (fine, (2,))):
         scratch += [pltpu.VMEM(size, jnp.float32) for size in stage_sizes(win, halos)]
     anywhere = pl.BlockSpec(memory_space=pl.ANY)

time: 38.3 us -> 38.5 us (level)
  no operation moved by 1% of the time
where the time goes in v6:
time: 38.5 us; the launch traced here: 38.4 us
  Pallas kernels  36.7 us (95%)
  other arithmetic  1.68 us (4%)
    pallas_call x1, Pallas kernels, on_device(): pl.pallas_call(functools.partial(cycle_kernel, sizes, (fine, mid)), out_s...  36.7 us
    mul x1, other arithmetic, on_device(): return OMEGA * scaled  1.68 us

profile of v6, /device:TPU:0, one launch (start us, length us, event | category | flops | bytes accessed | tf_op | source)
XLA Modules:
  0.0 38.4 jit_solution(5229124681182034776)
XLA Ops:
  0.0 36.7 %shard_map.37 = f32[32,16,128]{2,1,0:T(8,128)} custom-call(f32[32,16,128]{2,1,0:T(8,128)} %p_hbm.1, f32[32,16,128]{2,1,0:T(8,128)} %s_hbm.1, f32[32,16,128]{2,1,0:T(8,128)} %k_hbm.1), custom_call_target="tpu_custom_call" | custom-call | tf_op jit(solution)/shard_map/pallas_call | solution.py:674
  36.7 1.7 %broadcast_multiply_fusion = f32[32,16,128]{2,1,0:T(8,128)} fusion(f32[32,16,128]{2,1,0:T(8,128)} %shard_map.37), kind=kLoop, calls=%fused_computation | loop fusion | flops 65536 | bytes 524288 | tf_op jit(solution)/shard_map/mul | solution.py:683
